TPU v7x, 512 devices: a whole 4x4x16 slice. The times are simulated.
512 devices in a mesh: replica: 8 (over y, core), expert: 8 (over z_hi, x), fsdp: 8 (over z_lo).
Axes of the slice: x: 4, y: 4, z: 16 (z_hi: 2, z_lo: 8; z = z_hi * 8 + z_lo), core: 2. Of those that a mesh axis runs over, the one named last changes fastest.
Arguments:
- out_grad: bfloat16 [65536, 6144], P(('replica', 'expert', 'fsdp')), may hold values from -6 to 6
- saved_out: bfloat16 [8, 8, 8, 8, 34, 6144], P('replica', 'expert', 'fsdp'), may hold values from -6 to 6
- top_logits: float32 [65536, 2], P(('replica', 'expert', 'fsdp')), may hold values from -8 to 8
- expert_ids: int32 [65536, 2], P(('replica', 'expert', 'fsdp')), may hold values from 0 to 7, all different within a row; in each aligned block of 128 rows (0 to 127, 128 to 255, ...) at most 34 rows name the same one
- outer_params: float32 [128, 6144], P(('expert', 'fsdp')), may hold values from -6 to 6
- local_params: float32 [8, 128, 6144], P('replica', ('expert', 'fsdp')), may hold values from -6 to 6
- momentum: float32 [128, 6144], P(('expert', 'fsdp')), may hold values from -4 to 4
- fragment: int32 [8], P('replica'), may hold values from 0 to 3
- mix_rates: float32 [4], replicated, may hold values from 0.2 to 0.8
Outputs:
- logit_grad: float32 [65536, 2], P(('replica', 'expert', 'fsdp'))
- new_outer: float32 [128, 6144], P(('expert', 'fsdp'))
- new_momentum: float32 [128, 6144], P(('expert', 'fsdp'))
- mixed_params: float32 [8, 128, 6144], P('replica', ('expert', 'fsdp'))
Inputs may be any that keep to these rules, and one draw needn't show every extreme that they name: `expert_ids`: in each aligned block of 128 rows (the rows of one device) no expert is named by more than 34 rows, a bound that some block reaches; the two experts of a row differ.
All inputs are finite; a program needn't handle non-finite values.
Results may differ from a plain program's by a relative error of at most 0.0022.
The roundings to bfloat16 on the way count: a program that leaves them out, or rounds other values in their place, can miss the bound.
Values may be sent and summed in bfloat16 or wider, within the bound.
No kernel may reach another device: no remote copies, remote signals or barrier semaphores. Data moves between devices by JAX's collectives and lax.ppermute only.
A program may use at most 64 MiB of HBM per device.

v0:
```python
import jax
import jax.numpy as jnp
from jax import lax
from jax.sharding import PartitionSpec as P


def shards(
    out_grad,
    saved_out,
    top_logits,
    expert_ids,
    outer_params,
    local_params,
    momentum,
    fragment,
    mix_rates,
):
    tokens_here = out_grad.shape[0]
    width = out_grad.shape[1]
    owners = lax.axis_size("expert")
    local_experts = saved_out.shape[1]
    experts = owners * local_experts
    capacity = saved_out.shape[4]
    flat_ids = expert_ids.reshape(-1)
    onehot = (flat_ids[:, None] == jnp.arange(experts, dtype=jnp.int32)[None, :]).astype(jnp.int32)
    position = jnp.sum((jnp.cumsum(onehot, axis=0) - 1) * onehot, axis=1)
    slot_index = flat_ids * capacity + position
    lanes = jnp.arange(experts * capacity, dtype=jnp.int32)
    dispatch = (slot_index[None, :] == lanes[:, None]).astype(jnp.bfloat16)
    first = jax.nn.sigmoid(top_logits[:, 0] - top_logits[:, 1])
    probs = jnp.stack([first, 1.0 - first], axis=1)
    scaled = (probs[:, :, None] * out_grad[:, None, :].astype(jnp.float32)).astype(jnp.bfloat16)
    scaled = scaled.reshape(tokens_here * 2, width)
    payload = jnp.dot(dispatch, scaled, preferred_element_type=jnp.float32).astype(jnp.bfloat16)
    saved = saved_out.reshape(local_experts, owners, capacity, width)
    received = lax.all_to_all(
        payload.reshape(owners, local_experts, capacity, width),
        "expert",
        split_axis=0,
        concat_axis=0,
        tiled=True,
    )
    slot_products = jnp.einsum(
        "slcd,lscd->slc", received, saved, preferred_element_type=jnp.float32
    )
    returned = lax.all_to_all(slot_products, "expert", split_axis=0, concat_axis=0, tiled=True)
    products = returned.reshape(-1)
    pair = jnp.take(products, slot_index).reshape(tokens_here, 2)
    logit_grad = pair - probs * jnp.sum(pair, axis=1, keepdims=True)
    replicas = lax.axis_size("replica")
    pseudo = (
        lax.psum((outer_params - local_params[0]).astype(jnp.bfloat16), "replica").astype(
            jnp.float32
        )
        / replicas
    )
    total_sq = lax.psum(jnp.sum(pseudo * pseudo), ("expert", "fsdp"))
    entries = pseudo.shape[0] * lax.axis_size("expert") * lax.axis_size("fsdp") * width
    limit = 0.25 * jnp.sqrt(jnp.float32(entries) / replicas)
    scale = jnp.minimum(1.0, limit / jnp.sqrt(total_sq + 1e-06))
    clipped = scale * pseudo
    new_momentum = 0.9 * momentum + clipped
    new_outer = outer_params - 0.7 * (clipped + 0.9 * new_momentum)
    rate = jnp.take(mix_rates, fragment[0])
    mixed_params = local_params + rate * (new_outer[None] - local_params)
    return (logit_grad, new_outer, new_momentum, mixed_params)


def solution(mesh):
    in_specs = (
        P(("replica", "expert", "fsdp"), None),
        P("replica", "expert", "fsdp", None, None, None),
        P(("replica", "expert", "fsdp"), None),
        P(("replica", "expert", "fsdp"), None),
        P(("expert", "fsdp"), None),
        P("replica", ("expert", "fsdp"), None),
        P(("expert", "fsdp"), None),
        P("replica"),
        P(),
    )
    out_specs = (
        P(("replica", "expert", "fsdp"), None),
        P(("expert", "fsdp"), None),
        P(("expert", "fsdp"), None),
        P("replica", ("expert", "fsdp"), None),
    )
    return jax.shard_map(shards, mesh=mesh, in_specs=in_specs, out_specs=out_specs, check_vma=False)
```

profile of v0, /device:TPU:24, one launch (start us, length us, event | category | flops | bytes accessed | tf_op | source)
XLA Modules:
  0.0 455.2 jit_solution(10079811873026579928)
XLA Ops:
  0.6 0.8 copy.27
  1.6 0.1 eq.38
  1.7 6.8 %mul.92 = f32[128,2,6144]{2,1,0:T(2,128)} broadcast(bf16[128,6144]{1,0:T(8,128)(2,1)} %param.9), dimensions={0,2} | broadcast | bytes 7864320 | tf_op jit(solution)/shard_map/mul | solution.py:32
  8.5 8.3 %mul.93 = f32[256,6144]{1,0:T(8,128)} reshape(f32[128,2,6144]{2,1,0:T(2,128)} %mul.92) | data formatting | bytes 12582912 | tf_op jit(solution)/shard_map/mul | solution.py:32
  17.0 0.1 mul.90
  17.2 0.6 reduce-window.6
  17.8 0.2 slice_reduce_fusion
  18.1 3.9 convolution_convert_fusion
  22.1 2.4 reshape.99
  24.5 17.5 %all-to-all-start = ((bf16[8,1,34,6144]{3,2,1,0:T(8,128)(2,1)}), bf16[8,1,34,6144]{3,2,1,0:T(8,128)(2,1)}, u32[]{:S(2)}, u32[]{:S(2)}) async-start(bf16[8,1,34,6144]{3,2,1,0:T(8,128)(2,1)} %bitcast.30), calls=%async_computation | async-start | bytes 7864320 | tf_op jit(solution)/shard_map/all_to_all | solution.py:36
  42.1 23.0 %psum.14 = bf16[2,6144]{1,0:T(2,128)(2,1)S(1)} all-reduce(bf16[2,6144]{1,0:T(2,128)(2,1)S(1)} %fusion.10), channel_id=1, replica_groups=mesh['replica'=8,'expert'=8,'fsdp'=8] {'replica'}, use_global_device_ids=true, to_apply=%region_4.5 | all-reduce | flops 12288 | bytes 49152 | tf_op jit(solution)/shard_map/psum | solution.py:52
  65.1 0.7 fusion.7
  65.8 323.1 %psum.15 = f32[]{:T(128)} all-reduce(f32[]{:T(128)} %fusion.7), channel_id=1, replica_groups=mesh['replica'=8,'expert'=8,'fsdp'=8] {'expert','fsdp'}, use_global_device_ids=true, to_apply=%region_6.7 | all-reduce | flops 1 | bytes 8 | tf_op jit(solution)/shard_map/psum | solution.py:57
  389.9 0.6 dynamic-slice.2
  391.8 1.5 fusion.9
  393.3 3.1 bitcast_convert_fusion
  396.4 3.6 multiply_reduce_fusion
  400.0 0.7 copy.38
  400.7 35.6 %all-to-all-start.1 = ((f32[8,1,34]{2,1,0:T(1,128)}), f32[8,1,34]{2,1,0:T(1,128)S(1)}, u32[]{:S(2)}, u32[]{:S(2)}) async-start(f32[8,1,34]{2,1,0:T(1,128)} %bitcast.5), calls=%async_computation.1 | async-start | bytes 8192 | tf_op jit(solution)/shard_map/all_to_all | solution.py:46
  436.6 14.7 %all-to-all-done.1 = f32[8,1,34]{2,1,0:T(1,128)S(1)} async-done(((f32[8,1,34]{2,1,0:T(1,128)}), f32[8,1,34]{2,1,0:T(1,128)S(1)}, u32[]{:S(2)}, u32[]{:S(2)}) %all-to-all-start.1) | async-done | bytes 1120 | tf_op jit(solution)/shard_map/all_to_all | solution.py:46
  451.2 0.5 broadcast.113
  451.7 0.7 reduce.7
  452.5 1.9 gather_fusion
  454.7 0.6 multiply_subtract_fusion
  (34 shorter events, 1.3 us)
Async XLA Ops:
  8.5 8.3 %copy-start.4 = (f32[128,2]{0,1:T(2,128)S(1)}, f32[128,2]{0,1:T(2,128)}, u32[]{:S(2)}) copy-start(f32[128,2]{0,1:T(2,128)} %param.11) | copy-start | bytes 3076
  22.0 20.0 %copy-start.1 = (f32[1,2,6144]{2,1,0:T(2,128)S(1)}, f32[1,2,6144]{2,1,0:T(2,128)}, u32[]{:S(2)}) copy-start(f32[1,2,6144]{2,1,0:T(2,128)} %param.14) | copy-start | bytes 147460
  22.0 20.0 %copy-start.2 = (f32[2,6144]{1,0:T(2,128)S(1)}, f32[2,6144]{1,0:T(2,128)}, u32[]{:S(2)}) copy-start(f32[2,6144]{1,0:T(2,128)} %param.13) | copy-start | bytes 147460
  22.1 366.9 %copy-start.3 = (s32[128,2]{0,1:T(2,128)S(1)}, s32[128,2]{0,1:T(2,128)}, u32[]{:S(2)}) copy-start(s32[128,2]{0,1:T(2,128)} %param.12) | copy-start | bytes 3076
  22.1 367.8 %copy-start.5 = (f32[4]{0:T(128)S(1)}, f32[4]{0:T(128)}, u32[]{:S(2)}) copy-start(f32[4]{0:T(128)} %param.17) | copy-start | bytes 52
  24.5 368.8 %all-to-all-start = ((bf16[8,1,34,6144]{3,2,1,0:T(8,128)(2,1)}), bf16[8,1,34,6144]{3,2,1,0:T(8,128)(2,1)}, u32[]{:S(2)}, u32[]{:S(2)}) async-start(bf16[8,1,34,6144]{3,2,1,0:T(8,128)(2,1)} %bitcast.30), calls=%async_computation | async-start | bytes 7864320 | tf_op jit(solution)/shard_map/all_to_all | solution.py:36
  42.1 354.3 %copy-start = (bf16[1,1,1,8,34,6144]{5,3,4,2,1,0:T(8,128)(2,1)S(1)}, bf16[1,1,1,8,34,6144]{5,3,4,2,1,0:T(8,128)(2,1)}, u32[]{:S(2)}) copy-start(bf16[1,1,1,8,34,6144]{5,3,4,2,1,0:T(8,128)(2,1)} %param.10) | copy-start | bytes 10027012
  400.7 50.5 %all-to-all-start.1 = ((f32[8,1,34]{2,1,0:T(1,128)}), f32[8,1,34]{2,1,0:T(1,128)S(1)}, u32[]{:S(2)}, u32[]{:S(2)}) async-start(f32[8,1,34]{2,1,0:T(1,128)} %bitcast.5), calls=%async_computation.1 | async-start | bytes 8192 | tf_op jit(solution)/shard_map/all_to_all | solution.py:46
where the time goes:
time: 456 us; the launch traced here: 455 us
  blocking collectives  346 us (76%)
  starting transfers between devices  53.2 us (12%)
  local copies, waits for them, and re-layouts  23.6 us (5%)
  waiting for transfers between devices  14.7 us (3%)
  other arithmetic  10.9 us (2%)
    psum x1, blocking collectives, shards(): total_sq = lax.psum(jnp.sum(pseudo * pseudo), ('expert', 'fsdp'))  323 us
    all_to_all x1, starting transfers between devices, shards(): lax.all_to_all(slot_products, 'expert', split_axis=0, concat_axis=0, tile...  35.6 us
    psum x1, blocking collectives, shards(): lax.psum((outer_params - local_params[0]).astype(jnp.bfloat16), 'replica')  23 us
    all_to_all x1, starting transfers between devices, shards(): lax.all_to_all(payload.reshape(owners, local_experts, capacity, width), '...  17.5 us
    mul x3, local copies, waits for them, and re-layouts, shards(): probs[:, :, None] * out_grad[:, None, :].astype(jnp.float32)  15.3 us
    all_to_all x1, waiting for transfers between devices, shards(): lax.all_to_all(slot_products, 'expert', split_axis=0, concat_axis=0, tile...  14.7 us
  transfers between devices with their start and end apart: 2, of which 1 were waited for; matrix products, arithmetic and copies ran while one was open for 1% of the time, Pallas kernels for 0%

commit v1 on v0

v1 whole, which is shorter than its diff:
```python
import jax
import jax.numpy as jnp
from jax import lax
from jax.sharding import PartitionSpec as P

HEAD = 1536


def shards(
    out_grad,
    saved_out,
    top_logits,
    expert_ids,
    outer_params,
    local_params,
    momentum,
    fragment,
    mix_rates,
):
    tokens, width = out_grad.shape
    owners = lax.axis_size("expert")
    capacity = saved_out.shape[4]
    side = owners // 2
    block = side * capacity
    me = lax.axis_index("expert")
    half = me // side
    groups = [list(range(side)), list(range(side, owners))]
    across = [(e, (e + side) % owners) for e in range(owners)]

    def along_x(value):
        return lax.all_to_all(
            value, "expert", split_axis=0, concat_axis=0, axis_index_groups=groups, tiled=True
        )

    def over_z(value):
        return lax.ppermute(value, "expert", across)

    saved = saved_out.reshape(owners, capacity, width)
    far = lax.dynamic_slice_in_dim(saved, (1 - half) * side, side, 0)
    near = lax.dynamic_slice_in_dim(saved, half * side, side, 0)

    head = over_z(far[:, :, :HEAD].reshape(block, HEAD))
    rest = over_z(along_x(far[:, :, HEAD:]).reshape(block, width - HEAD))
    near_rows = along_x(near).reshape(block, width)
    head_rows = along_x(head.reshape(side, capacity, HEAD)).reshape(block, HEAD)

    count = jnp.arange(owners, dtype=jnp.int32)
    named = [(expert_ids[:, k : k + 1] == count[None, :]).astype(jnp.bfloat16) for k in range(2)]
    row = lax.broadcasted_iota(jnp.int32, (tokens, tokens), 0)
    col = lax.broadcasted_iota(jnp.int32, (tokens, tokens), 1)
    before = jnp.dot(
        (col < row).astype(jnp.bfloat16), named[0] + named[1], preferred_element_type=jnp.float32
    )
    slot = [
        expert_ids[:, k] * capacity
        + jnp.sum(before * named[k].astype(jnp.float32), axis=1).astype(jnp.int32)
        for k in range(2)
    ]
    slot = jnp.concatenate(slot)
    lanes = jnp.arange(block, dtype=jnp.int32)
    near_mask = (slot - half * block)[:, None] == lanes[None, :]
    far_mask = (slot - (1 - half) * block)[:, None] == lanes[None, :]

    first = jax.nn.sigmoid(top_logits[:, 0] - top_logits[:, 1])
    second = 1.0 - first
    grads = out_grad.astype(jnp.float32)
    payload = jnp.concatenate(
        [
            (first[:, None] * grads).astype(jnp.bfloat16),
            (second[:, None] * grads).astype(jnp.bfloat16),
        ]
    )

    def inner(a, b):
        return lax.dot_general(
            a, b, (((1,), (1,)), ((), ())), preferred_element_type=jnp.float32
        )

    near_products = jnp.where(near_mask, inner(payload, near_rows), 0.0)
    far_products = inner(payload[:, :HEAD], head_rows) + inner(payload[:, HEAD:], rest)
    pair = jnp.sum(near_products, axis=1) + jnp.sum(jnp.where(far_mask, far_products, 0.0), axis=1)
    pair0, pair1 = pair[:tokens], pair[tokens:]
    both = pair0 + pair1
    logit_grad = jnp.stack([pair0 - first * both, pair1 - second * both], axis=1)

    replicas = lax.axis_size("replica")
    pseudo = (
        lax.psum((outer_params - local_params[0]).astype(jnp.bfloat16), "replica").astype(
            jnp.float32
        )
        / replicas
    )
    total_sq = lax.psum(jnp.sum(pseudo * pseudo), ("expert", "fsdp"))
    entries = pseudo.shape[0] * lax.axis_size("expert") * lax.axis_size("fsdp") * width
    limit = 0.25 * jnp.sqrt(jnp.float32(entries) / replicas)
    scale = jnp.minimum(1.0, limit / jnp.sqrt(total_sq + 1e-06))
    clipped = scale * pseudo
    new_momentum = 0.9 * momentum + clipped
    new_outer = outer_params - 0.7 * (clipped + 0.9 * new_momentum)
    rate = jnp.take(mix_rates, fragment[0])
    mixed_params = local_params + rate * (new_outer[None] - local_params)
    return (logit_grad, new_outer, new_momentum, mixed_params)


def solution(mesh):
    in_specs = (
        P(("replica", "expert", "fsdp"), None),
        P("replica", "expert", "fsdp", None, None, None),
        P(("replica", "expert", "fsdp"), None),
        P(("replica", "expert", "fsdp"), None),
        P(("expert", "fsdp"), None),
        P("replica", ("expert", "fsdp"), None),
        P(("expert", "fsdp"), None),
        P("replica"),
        P(),
    )
    out_specs = (
        P(("replica", "expert", "fsdp"), None),
        P(("expert", "fsdp"), None),
        P(("expert", "fsdp"), None),
        P("replica", ("expert", "fsdp"), None),
    )
    return jax.shard_map(shards, mesh=mesh, in_specs=in_specs, out_specs=out_specs, check_vma=False)
```

time: 456 us -> 373 us (0.82)
  blocking collectives: 346 us -> 210 us
  waiting for transfers between devices: 14.7 us -> 48.2 us
  starting transfers between devices: 53.2 us -> 78.2 us
  other arithmetic: 10.9 us -> 6.17 us
    psum x1, blocking collectives: 323 us -> 188 us  [shards(): total_sq = lax.psum(jnp.sum(pseudo * pseudo), ('expert', 'fsdp'))]
    ppermute x0 -> x2, waiting for transfers between devices: none -> 35.9 us  [over_z(): return lax.ppermute(value, 'expert', across)]
    ppermute x0 -> x2, starting transfers between devices: none -> 34.9 us  [over_z(): return lax.ppermute(value, 'expert', across)]
    mul x5 -> x0, local copies, waits for them, and re-layouts: 15.6 us -> none  [the longest x3 15.3 us: shards(): probs[:, :, None] * out_grad[:, None, :].astype(jnp.float32)]
    all_to_all x2 -> x3, starting transfers between devices: 53.2 us -> 43.3 us  [along_x(): lax.all_to_all(value, 'expert', split_axis=0, concat_axis=0, axis_index_g...]
    dynamic_slice x0 -> x2, local copies, waits for them, and re-layouts: none -> 7.23 us  [the longest x1 5.03 us: shards(): far = lax.dynamic_slice_in_dim(saved, (1 - half) * side, side, 0)]
    reshape x2 -> x5, local copies, waits for them, and re-layouts: 2.52 us -> 9.24 us  [the longest x2 3.83 us: shards(): head_rows = along_x(head.reshape(side, capacity, HEAD)).reshape(block, HEAD)]
    unnamed x2 -> x0, other arithmetic: 6.69 us -> none
  transfers between devices with their start and end apart: 2 -> 5, of which waited for: 1 -> 2; matrix products, arithmetic and copies ran while one was open for 1% -> 6% of each run, Pallas kernels for 0% -> 0%
where the time goes in v1:
time: 373 us; the launch traced here: 371 us
  blocking collectives  210 us (56%)
  starting transfers between devices  78.2 us (21%)
  waiting for transfers between devices  48.2 us (13%)
  local copies, waits for them, and re-layouts  19.2 us (5%)
  other arithmetic  6.17 us (2%)
  matrix products  6.02 us (2%)
    psum x1, blocking collectives, shards(): total_sq = lax.psum(jnp.sum(pseudo * pseudo), ('expert', 'fsdp'))  188 us
    all_to_all x3, starting transfers between devices, along_x(): lax.all_to_all(value, 'expert', split_axis=0, concat_axis=0, axis_index_g...  43.3 us
    ppermute x2, waiting for transfers between devices, over_z(): return lax.ppermute(value, 'expert', across)  35.9 us
    ppermute x2, starting transfers between devices, over_z(): return lax.ppermute(value, 'expert', across)  34.9 us
    psum x1, blocking collectives, shards(): lax.psum((outer_params - local_params[0]).astype(jnp.bfloat16), 'replica')  22.1 us
    all_to_all x3, waiting for transfers between devices, along_x(): lax.all_to_all(value, 'expert', split_axis=0, concat_axis=0, axis_index_g...  12.3 us
  transfers between devices with their start and end apart: 5, of which 2 were waited for; matrix products, arithmetic and copies ran while one was open for 6% of the time, Pallas kernels for 0%

profile of v1, /device:TPU:24, one launch (start us, length us, event | category | flops | bytes accessed | tf_op | source)
XLA Modules:
  0.0 370.9 jit_solution(14496972195754333049)
XLA Ops:
  0.7 5.0 %dynamic-slice_bitcast_fusion = (bf16[4,34,6144]{2,0,1:T(4,128)(2,1)S(1)}, bf16[4,34,6144]{2,0,1:T(4,128)(2,1)S(1)}) fusion(bf16[1,1,1,8,34,6144]{5,3,4,2,1,0:T(8,128)(2,1)} %param.10, s32[]{:T(128)S(6)} %select_n.29, s32[]{:T(128)S(6)} %select_n.27), kind=kLoop, calls=%fused_computation.12 | loop fusion | bytes 6684680 | tf_op jit(solution)/shard_map/dynamic_slice | solution.py:39
  6.1 1.4 copy.18
  7.5 4.3 %all-to-all-start.2 = ((bf16[4,34,4608]{2,1,0:T(8,128)(2,1)}), bf16[4,34,4608]{2,1,0:T(8,128)(2,1)}, u32[]{:S(2)}, u32[]{:S(2)}) async-start(bf16[4,34,4608]{2,1,0:T(8,128)(2,1)} %copy.18), calls=%async_computation.2 | async-start | bytes 2949120 | tf_op jit(solution)/shard_map/all_to_all | solution.py:31
  12.2 0.9 reshape.71
  13.0 15.7 %collective-permute-start = (bf16[136,1536]{1,0:T(8,128)(2,1)}, bf16[136,1536]{1,0:T(8,128)(2,1)}, u32[]{:S(2)}, u32[]{:S(2)}) collective-permute-start(bf16[136,1536]{1,0:T(8,128)(2,1)} %reshape.71), channel_id=1, source_target_pairs={{0,32},{8,40},{16,48},{24,56},{32,0},{40,8},{48,16},{56,24},{1,33}... | collective-permute-start | bytes 1253384 | tf_op jit(solution)/shard_map/ppermute | solution.py:36
  28.8 22.1 %psum.14 = bf16[2,6144]{1,0:T(2,128)(2,1)S(1)} all-reduce(bf16[2,6144]{1,0:T(2,128)(2,1)S(1)} %fusion.30), channel_id=1, replica_groups=mesh['replica'=8,'expert'=8,'fsdp'=8] {'replica'}, use_global_device_ids=true, to_apply=%region_4.5 | all-reduce | flops 12288 | bytes 49152 | tf_op jit(solution)/shard_map/psum | solution.py:88
  51.0 0.7 fusion.27
  51.6 3.3 fusion
  54.9 188.1 %psum.15 = f32[]{:T(128)} all-reduce(f32[]{:T(128)} %fusion.27), channel_id=1, replica_groups=mesh['replica'=8,'expert'=8,'fsdp'=8] {'expert','fsdp'}, use_global_device_ids=true, to_apply=%region_6.7 | all-reduce | flops 1 | bytes 8 | tf_op jit(solution)/shard_map/psum | solution.py:93
  243.7 2.2 copy.16
  245.9 0.6 dynamic-slice.4
  248.0 1.9 reshape.72
  249.9 34.2 %all-to-all-start.1 = ((bf16[4,34,1536]{2,1,0:T(8,128)(2,1)}), bf16[4,34,1536]{2,1,0:T(8,128)(2,1)}, u32[]{:S(2)}, u32[]{:S(2)}) async-start(bf16[4,34,1536]{2,1,0:T(8,128)(2,1)} %reshape.72), calls=%async_computation.1 | async-start | bytes 983040 | tf_op jit(solution)/shard_map/all_to_all | solution.py:31
  284.1 2.8 reshape.74
  286.9 19.2 %collective-permute-start.1 = (bf16[136,4608]{1,0:T(8,128)(2,1)}, bf16[136,4608]{1,0:T(8,128)(2,1)}, u32[]{:S(2)}, u32[]{:S(2)}) collective-permute-start(bf16[136,4608]{1,0:T(8,128)(2,1)} %reshape.74), channel_id=1, source_target_pairs={{0,32},{8,40},{16,48},{24,56},{32,0},{40,8},{48,16},{56,24},{1,33}... | collective-permute-start | bytes 3760136 | tf_op jit(solution)/shard_map/ppermute | solution.py:36
  306.2 4.8 %all-to-all-start = ((bf16[4,34,6144]{2,1,0:T(8,128)(2,1)}), bf16[4,34,6144]{2,1,0:T(8,128)(2,1)S(1)}, u32[]{:S(2)}, u32[]{:S(2)}) async-start(bf16[4,34,6144]{2,1,0:T(8,128)(2,1)} %copy.16), calls=%async_computation | async-start | bytes 3932160 | tf_op jit(solution)/shard_map/all_to_all | solution.py:31
  311.0 1.6 fusion.29
  312.6 1.9 reshape.73
  314.5 12.3 %all-to-all-done = bf16[4,34,6144]{2,1,0:T(8,128)(2,1)S(1)} async-done(((bf16[4,34,6144]{2,1,0:T(8,128)(2,1)}), bf16[4,34,6144]{2,1,0:T(8,128)(2,1)S(1)}, u32[]{:S(2)}, u32[]{:S(2)}) %all-to-all-start) | async-done | bytes 1671200 | tf_op jit(solution)/shard_map/all_to_all | solution.py:31
  326.8 1.7 reshape.70
  328.5 3.2 fusion.15
  331.7 35.9 %collective-permute-done.1 = bf16[136,4608]{1,0:T(8,128)(2,1)} collective-permute-done((bf16[136,4608]{1,0:T(8,128)(2,1)}, bf16[136,4608]{1,0:T(8,128)(2,1)}, u32[]{:S(2)}, u32[]{:S(2)}) %collective-permute-start.1) | collective-permute-done | bytes 1253408 | tf_op jit(solution)/shard_map/ppermute | solution.py:36
  367.6 2.2 fusion.6
  370.3 0.6 pad_maximum_fusion
  (31 shorter events, 1.4 us)
Async XLA Ops:
  7.5 242.4 %all-to-all-start.2 = ((bf16[4,34,4608]{2,1,0:T(8,128)(2,1)}), bf16[4,34,4608]{2,1,0:T(8,128)(2,1)}, u32[]{:S(2)}, u32[]{:S(2)}) async-start(bf16[4,34,4608]{2,1,0:T(8,128)(2,1)} %copy.18), calls=%async_computation.2 | async-start | bytes 2949120 | tf_op jit(solution)/shard_map/all_to_all | solution.py:31
  11.9 16.9 %copy-start.6 = (f32[128,2]{0,1:T(2,128)S(1)}, f32[128,2]{0,1:T(2,128)}, u32[]{:S(2)}) copy-start(f32[128,2]{0,1:T(2,128)} %param.11) | copy-start | bytes 3076
  11.9 16.9 %copy-start.3 = (f32[1,2,6144]{2,1,0:T(2,128)S(1)}, f32[1,2,6144]{2,1,0:T(2,128)}, u32[]{:S(2)}) copy-start(f32[1,2,6144]{2,1,0:T(2,128)} %param.14) | copy-start | bytes 147460
  11.9 16.9 %copy-start.4 = (f32[2,6144]{1,0:T(2,128)S(1)}, f32[2,6144]{1,0:T(2,128)}, u32[]{:S(2)}) copy-start(f32[2,6144]{1,0:T(2,128)} %param.13) | copy-start | bytes 147460
  13.0 234.9 %collective-permute-start = (bf16[136,1536]{1,0:T(8,128)(2,1)}, bf16[136,1536]{1,0:T(8,128)(2,1)}, u32[]{:S(2)}, u32[]{:S(2)}) collective-permute-start(bf16[136,1536]{1,0:T(8,128)(2,1)} %reshape.71), channel_id=1, source_target_pairs={{0,32},{8,40},{16,48},{24,56},{32,0},{40,8},{48,16},{56,24},{1,33}... | collective-permute-start | bytes 1253384 | tf_op jit(solution)/shard_map/ppermute | solution.py:36
  51.0 3.9 %copy-start.2 = (bf16[2,6144]{1,0:T(2,128)(2,1)}, bf16[2,6144]{1,0:T(2,128)(2,1)S(1)}, u32[]{:S(2)}) copy-start(bf16[2,6144]{1,0:T(2,128)(2,1)S(1)} %psum.14) | copy-start | bytes 73732
  243.6 2.2 copy-start.7
  243.7 4.1 %copy-start.5 = (s32[128,2]{0,1:T(2,128)S(1)}, s32[128,2]{0,1:T(2,128)}, u32[]{:S(2)}) copy-start(s32[128,2]{0,1:T(2,128)} %param.12) | copy-start | bytes 3076
  249.9 56.3 %all-to-all-start.1 = ((bf16[4,34,1536]{2,1,0:T(8,128)(2,1)}), bf16[4,34,1536]{2,1,0:T(8,128)(2,1)}, u32[]{:S(2)}, u32[]{:S(2)}) async-start(bf16[4,34,1536]{2,1,0:T(8,128)(2,1)} %reshape.72), calls=%async_computation.1 | async-start | bytes 983040 | tf_op jit(solution)/shard_map/all_to_all | solution.py:31
  286.9 80.7 %collective-permute-start.1 = (bf16[136,4608]{1,0:T(8,128)(2,1)}, bf16[136,4608]{1,0:T(8,128)(2,1)}, u32[]{:S(2)}, u32[]{:S(2)}) collective-permute-start(bf16[136,4608]{1,0:T(8,128)(2,1)} %reshape.74), channel_id=1, source_target_pairs={{0,32},{8,40},{16,48},{24,56},{32,0},{40,8},{48,16},{56,24},{1,33}... | collective-permute-start | bytes 3760136 | tf_op jit(solution)/shard_map/ppermute | solution.py:36
  306.2 20.6 %all-to-all-start = ((bf16[4,34,6144]{2,1,0:T(8,128)(2,1)}), bf16[4,34,6144]{2,1,0:T(8,128)(2,1)S(1)}, u32[]{:S(2)}, u32[]{:S(2)}) async-start(bf16[4,34,6144]{2,1,0:T(8,128)(2,1)} %copy.16), calls=%async_computation | async-start | bytes 3932160 | tf_op jit(solution)/shard_map/all_to_all | solution.py:31
  328.5 39.1 %copy-start = (bf16[128,6144]{1,0:T(8,128)(2,1)S(1)}, bf16[128,6144]{1,0:T(8,128)(2,1)}, u32[]{:S(2)}) copy-start(bf16[128,6144]{1,0:T(8,128)(2,1)} %get-tuple-element.25) | copy-start | bytes 4718596
  331.7 38.1 %copy-start.1 = (bf16[136,1536]{1,0:T(8,128)(2,1)S(1)}, bf16[136,1536]{1,0:T(8,128)(2,1)}, u32[]{:S(2)}) copy-start(bf16[136,1536]{1,0:T(8,128)(2,1)} %reshape.73) | copy-start | bytes 1253380

commit v2 on v1

--- a/solution.py
+++ b/solution.py
@@ -3,7 +3,10 @@
 from jax import lax
 from jax.sharding import PartitionSpec as P
 
-HEAD = 1536
+CUTS = (0, 1536, 3072, 4096, 5120, 6144)
+EARLY = 2
+FLIGHT = 2
+AXES = ("replica", "expert", "fsdp")
 
 
 def shards(
@@ -18,12 +21,11 @@
     mix_rates,
 ):
     tokens, width = out_grad.shape
-    owners = lax.axis_size("expert")
+    replicas, owners, runs = (lax.axis_size(axis) for axis in AXES)
     capacity = saved_out.shape[4]
     side = owners // 2
     block = side * capacity
-    me = lax.axis_index("expert")
-    half = me // side
+    half = lax.axis_index("expert") // side
     groups = [list(range(side)), list(range(side, owners))]
     across = [(e, (e + side) % owners) for e in range(owners)]
 
@@ -35,14 +37,72 @@
     def over_z(value):
         return lax.ppermute(value, "expert", across)
 
+    def swap_x(value, step):
+        return lax.ppermute(value, "expert", [(e, e ^ step) for e in range(owners)])
+
+    def place(r, z, x):
+        return (r * owners + z // runs * side + x) * runs + z % runs
+
+    depth = 2 * runs
+
+    def along_z(value, start):
+        return lax.ppermute(
+            value,
+            AXES,
+            [
+                (place(r, z, x), place(r, (z + start + r) % depth, x))
+                for r in range(replicas)
+                for z in range(depth)
+                for x in range(side)
+            ],
+        )
+
     saved = saved_out.reshape(owners, capacity, width)
-    far = lax.dynamic_slice_in_dim(saved, (1 - half) * side, side, 0)
-    near = lax.dynamic_slice_in_dim(saved, half * side, side, 0)
+    other = 1 - half
 
-    head = over_z(far[:, :, :HEAD].reshape(block, HEAD))
-    rest = over_z(along_x(far[:, :, HEAD:]).reshape(block, width - HEAD))
+    def part(which, first, last, rows=saved):
+        return lax.dynamic_slice(
+            rows, (which * side, 0, first), (side, capacity, last - first)
+        )
+
+    pseudo = (
+        lax.psum((outer_params - local_params[0]).astype(jnp.bfloat16), "replica").astype(
+            jnp.float32
+        )
+        / replicas
+    )
+    own_sq = jnp.sum(pseudo * pseudo).reshape(1, 1)
+    after_sum, own_sq = lax.optimization_barrier((saved, own_sq))
+
+    pieces = len(CUTS) - 1
+    middle = EARLY + 1
+    spread = {}
+    for first, last in ((EARLY, middle), (middle, pieces)):
+        rows = along_x(part(other, CUTS[first], CUTS[last], after_sum))
+        for i in range(first, last):
+            spread[i] = rows[:, :, CUTS[i] - CUTS[first] : CUTS[i + 1] - CUTS[first]]
+    came = []
+    for i in range(pieces):
+        rows = part(other, CUTS[i], CUTS[i + 1]) if i < EARLY else spread[i]
+        rows = rows.reshape(block, CUTS[i + 1] - CUTS[i])
+        if i >= FLIGHT:
+            rows, came[i - FLIGHT] = lax.optimization_barrier((rows, came[i - FLIGHT]))
+        came.append(over_z(rows))
+        if i == 0:
+            came[0], own_sq = lax.optimization_barrier((came[0], own_sq))
+            window = along_z(own_sq, 0) + along_z(own_sq, replicas)
+
+    after_early, came[1], window = lax.optimization_barrier((after_sum, came[1], window))
+    window = lax.psum(window, "replica")
+    window = window + swap_x(window, 1)
+    total_sq = (window + swap_x(window, 2))[0, 0]
+
+    near = lax.dynamic_slice_in_dim(after_early, half * side, side, 0)
     near_rows = along_x(near).reshape(block, width)
-    head_rows = along_x(head.reshape(side, capacity, HEAD)).reshape(block, HEAD)
+    crossed = jnp.concatenate(came[:EARLY], axis=1).reshape(side, capacity, CUTS[EARLY])
+    crossed = along_x(crossed).reshape(block, CUTS[EARLY])
+    far_rows = [crossed] + came[EARLY:]
+    cuts = (0,) + CUTS[EARLY:]
 
     count = jnp.arange(owners, dtype=jnp.int32)
     named = [(expert_ids[:, k : k + 1] == count[None, :]).astype(jnp.bfloat16) for k in range(2)]
@@ -51,15 +111,16 @@
     before = jnp.dot(
         (col < row).astype(jnp.bfloat16), named[0] + named[1], preferred_element_type=jnp.float32
     )
-    slot = [
-        expert_ids[:, k] * capacity
-        + jnp.sum(before * named[k].astype(jnp.float32), axis=1).astype(jnp.int32)
-        for k in range(2)
-    ]
-    slot = jnp.concatenate(slot)
+    slot = jnp.concatenate(
+        [
+            expert_ids[:, k] * capacity
+            + jnp.sum(before * named[k].astype(jnp.float32), axis=1).astype(jnp.int32)
+            for k in range(2)
+        ]
+    )
     lanes = jnp.arange(block, dtype=jnp.int32)
     near_mask = (slot - half * block)[:, None] == lanes[None, :]
-    far_mask = (slot - (1 - half) * block)[:, None] == lanes[None, :]
+    far_mask = (slot - other * block)[:, None] == lanes[None, :]
 
     first = jax.nn.sigmoid(top_logits[:, 0] - top_logits[:, 1])
     second = 1.0 - first
@@ -76,22 +137,19 @@
             a, b, (((1,), (1,)), ((), ())), preferred_element_type=jnp.float32
         )
 
-    near_products = jnp.where(near_mask, inner(payload, near_rows), 0.0)
-    far_products = inner(payload[:, :HEAD], head_rows) + inner(payload[:, HEAD:], rest)
-    pair = jnp.sum(near_products, axis=1) + jnp.sum(jnp.where(far_mask, far_products, 0.0), axis=1)
+    def picked(mask, rows, first, last):
+        return jnp.sum(jnp.where(mask, inner(payload[:, first:last], rows), 0.0), axis=1)
+
+    pair = picked(near_mask, near_rows, 0, width)
+    for i, rows in enumerate(far_rows):
+        if i == len(far_rows) - 1:
+            rows, pair = lax.optimization_barrier((rows, pair))
+        pair = pair + picked(far_mask, rows, cuts[i], cuts[i + 1])
     pair0, pair1 = pair[:tokens], pair[tokens:]
     both = pair0 + pair1
     logit_grad = jnp.stack([pair0 - first * both, pair1 - second * both], axis=1)
 
-    replicas = lax.axis_size("replica")
-    pseudo = (
-        lax.psum((outer_params - local_params[0]).astype(jnp.bfloat16), "replica").astype(
-            jnp.float32
-        )
-        / replicas
-    )
-    total_sq = lax.psum(jnp.sum(pseudo * pseudo), ("expert", "fsdp"))
-    entries = pseudo.shape[0] * lax.axis_size("expert") * lax.axis_size("fsdp") * width
+    entries = pseudo.shape[0] * owners * runs * width
     limit = 0.25 * jnp.sqrt(jnp.float32(entries) / replicas)
     scale = jnp.minimum(1.0, limit / jnp.sqrt(total_sq + 1e-06))
     clipped = scale * pseudo

time: 373 us -> 200 us (0.54)
  the two profiles are of different devices: /device:TPU:24 before, /device:TPU:34 now
where the time goes in v2:
time: 200 us; the launch traced here: 199 us
  starting transfers between devices  80.7 us (40%)
  blocking collectives  40.9 us (20%)
  local copies, waits for them, and re-layouts  31.2 us (16%)
  waiting for transfers between devices  23.8 us (12%)
  other arithmetic  8.8 us (4%)
  matrix products  8.23 us (4%)
  between operations  5.27 us (3%)
    ppermute x5, starting transfers between devices, over_z(): return lax.ppermute(value, 'expert', across)  36.4 us
    psum x1, blocking collectives, shards(): lax.psum((outer_params - local_params[0]).astype(jnp.bfloat16), 'replica')  27.2 us
    all_to_all x4, starting transfers between devices, along_x(): lax.all_to_all(value, 'expert', split_axis=0, concat_axis=0, axis_index_g...  21.9 us
    ppermute x2, starting transfers between devices, along_z(): lax.ppermute(value, AXES, [(place(r, z, x), place(r, (z + start + r) % de...  13.9 us
    psum x1, blocking collectives, shards(): window = lax.psum(window, 'replica')  13.7 us
    all_to_all x4, waiting for transfers between devices, along_x(): lax.all_to_all(value, 'expert', split_axis=0, concat_axis=0, axis_index_g...  10.7 us
    ppermute x5, waiting for transfers between devices, over_z(): return lax.ppermute(value, 'expert', across)  10.5 us
    ppermute x2, starting transfers between devices, swap_x(): return lax.ppermute(value, 'expert', [(e, e ^ step) for e in range(owners)])  8.36 us
  transfers between devices with their start and end apart: 13, of which 5 were waited for; matrix products, arithmetic and copies ran while one was open for 22% of the time, Pallas kernels for 0%

profile of v2, /device:TPU:34, one launch (start us, length us, event | category | flops | bytes accessed | tf_op | source)
XLA Modules:
  0.0 198.8 jit_solution(17671338279787377891)
XLA Ops:
  3.5 14.8 %collective-permute-start = (bf16[136,1536]{1,0:T(8,128)(2,1)}, bf16[136,1536]{1,0:T(8,128)(2,1)}, u32[]{:S(2)}, u32[]{:S(2)}) collective-permute-start(bf16[136,1536]{1,0:T(8,128)(2,1)} %reshape.97), channel_id=1, source_target_pairs={{0,32},{8,40},{16,48},{24,56},{32,0},{40,8},{48,16},{56,24},{1,33}... | collective-permute-start | bytes 1253384 | tf_op jit(solution)/shard_map/ppermute | solution.py:38
  21.3 5.7 %copy.23 = bf16[1,1,1,8,34,6144]{5,4,3,2,1,0:T(8,128)(2,1)} copy(bf16[1,1,1,8,34,6144]{5,3,4,2,1,0:T(8,128)(2,1)} %param.10) | data formatting | bytes 6684672 | tf_op args[1]
  27.0 27.2 %psum.14 = bf16[2,6144]{1,0:T(2,128)(2,1)S(1)} all-reduce(bf16[2,6144]{1,0:T(2,128)(2,1)S(1)} %fusion.32), channel_id=1, replica_groups=mesh['replica'=8,'expert'=8,'fsdp'=8] {'replica'}, use_global_device_ids=true, to_apply=%region_0.1 | all-reduce | flops 12288 | bytes 49152 | tf_op jit(solution)/shard_map/psum | solution.py:69
  56.6 4.8 %all-to-all-start.1 = ((bf16[4,34,1024]{2,1,0:T(8,128)(2,1)}), bf16[4,34,1024]{2,1,0:T(8,128)(2,1)S(1)}, u32[]{:S(2)}, u32[]{:S(2)}) async-start(bf16[4,34,1024]{2,1,0:T(8,128)(2,1)} %constant_dynamic-slice_fusion.3), calls=%async_computation.1 | async-start | bytes 655360 | tf_op jit(solution)/shard_map/all_to_all | solution.py:33
  63.4 2.1 %fusion.1 = (bf16[128,6144]{1,0:T(8,128)(2,1)S(1)}, bf16[128,6144]{1,0:T(8,128)(2,1)S(1)}) fusion(bf16[128,6144]{1,0:T(8,128)(2,1)} %param.9, f32[128]{0:T(128)S(1)} %get-tuple-element.50, f32[128]{0:T(128)S(1)} %bitcast.54), kind=kLoop, calls=%fused_computation.13 | loop fusion | flops 3932160 | bytes 4719616 | tf_op jit(solution)/shard_map/convert_element_type | solution.py:131
  67.0 5.6 %all-to-all-start = ((bf16[4,34,2048]{2,1,0:T(8,128)(2,1)}), bf16[4,34,2048]{2,1,0:T(8,128)(2,1)}, u32[]{:S(2)}, u32[]{:S(2)}) async-start(bf16[4,34,2048]{2,1,0:T(8,128)(2,1)} %constant_dynamic-slice_fusion.4), calls=%async_computation | async-start | bytes 1310720 | tf_op jit(solution)/shard_map/all_to_all | solution.py:33
  78.6 4.6 %collective-permute-done = bf16[136,1536]{1,0:T(8,128)(2,1)} collective-permute-done((bf16[136,1536]{1,0:T(8,128)(2,1)}, bf16[136,1536]{1,0:T(8,128)(2,1)}, u32[]{:S(2)}, u32[]{:S(2)}) %collective-permute-start) | collective-permute-done | bytes 417824 | tf_op jit(solution)/shard_map/ppermute | solution.py:38
  85.0 12.2 %collective-permute-start.5 = (f32[1,1]{1,0:T(1,128)}, f32[1,1]{1,0:T(1,128)}, u32[]{:S(2)}, u32[]{:S(2)}) collective-permute-start(f32[1,1]{1,0:T(1,128)} %bitcast.2), channel_id=1, source_target_pairs={{0,32},{8,40},{16,48},{24,56},{1,33},{9,41},{17,49},{25,57},{2,34}... | collective-permute-start | bytes 20 | tf_op jit(solution)/shard_map/ppermute | solution.py:49
  100.8 2.6 %collective-permute-start.1 = (bf16[136,1024]{1,0:T(8,128)(2,1)}, bf16[136,1024]{1,0:T(8,128)(2,1)}, u32[]{:S(2)}, u32[]{:S(2)}) collective-permute-start(bf16[136,1024]{1,0:T(8,128)(2,1)} %reshape.96), channel_id=1, source_target_pairs={{0,32},{8,40},{16,48},{24,56},{32,0},{40,8},{48,16},{56,24},{1,33}... | collective-permute-start | bytes 835592 | tf_op jit(solution)/shard_map/ppermute | solution.py:38
  104.2 12.0 %collective-permute-start.6 = (bf16[136,1024]{1,0:T(8,128)(2,1)}, bf16[136,1024]{1,0:T(8,128)(2,1)S(1)}, u32[]{:S(2)}, u32[]{:S(2)}) collective-permute-start(bf16[136,1024]{1,0:T(8,128)(2,1)} %reshape.98), channel_id=1, source_target_pairs={{0,32},{8,40},{16,48},{24,56},{32,0},{40,8},{48,16},{56,24},{1,33}... | collective-permute-start | bytes 835592 | tf_op jit(solution)/shard_map/ppermute | solution.py:38
  117.4 13.7 %psum.15 = f32[1,1]{1,0:T(1,128)} all-reduce(f32[1,1]{1,0:T(1,128)S(6)} %add.79), channel_id=1, replica_groups=mesh['replica'=8,'expert'=8,'fsdp'=8] {'replica'}, use_global_device_ids=true, to_apply=%region_9.10 | all-reduce | flops 1 | bytes 8 | tf_op jit(solution)/shard_map/psum | solution.py:96
  131.2 2.4 %collective-permute-start.7 = (f32[1,1]{1,0:T(1,128)}, f32[1,1]{1,0:T(1,128)}, u32[]{:S(2)}, u32[]{:S(2)}) collective-permute-start(f32[1,1]{1,0:T(1,128)} %psum.15), channel_id=1, source_target_pairs={{0,8},{8,0},{16,24},{24,16},{32,40},{40,32},{48,56},{56,48},{1,9},... | collective-permute-start | bytes 20 | tf_op jit(solution)/shard_map/ppermute | solution.py:41
  135.7 2.3 %reshape.101 = bf16[4,34,3072]{2,1,0:T(8,128)(2,1)} reshape(bf16[136,3072]{1,0:T(8,128)(2,1)} %pad_maximum_fusion.6) | data formatting | bytes 1671168 | tf_op jit(solution)/shard_map/reshape | solution.py:102
  138.1 5.7 %all-to-all-start.3 = ((bf16[4,34,3072]{2,1,0:T(8,128)(2,1)}), bf16[4,34,3072]{2,1,0:T(8,128)(2,1)}, u32[]{:S(2)}, u32[]{:S(2)}) async-start(bf16[4,34,3072]{2,1,0:T(8,128)(2,1)} %reshape.101), calls=%async_computation.3 | async-start | bytes 1966080 | tf_op jit(solution)/shard_map/all_to_all | solution.py:33
  143.7 3.0 %constant_dynamic-slice_fusion = bf16[4,34,6144]{2,1,0:T(8,128)(2,1)} fusion(bf16[8,34,6144]{2,1,0:T(8,128)(2,1)} %bitcast.53, s32[]{:T(128)S(6)} %select_n.40), kind=kLoop, calls=%fused_computation.57 | loop fusion | bytes 3342340 | tf_op jit(solution)/shard_map/dynamic_slice | solution.py:100
  148.0 5.9 %collective-permute-start.8 = (f32[1,1]{1,0:T(1,128)}, f32[1,1]{1,0:T(1,128)}, u32[]{:S(2)}, u32[]{:S(2)}) collective-permute-start(f32[1,1]{1,0:T(1,128)} %add.87), channel_id=1, source_target_pairs={{0,16},{8,24},{16,0},{24,8},{32,48},{40,56},{48,32},{56,40},{1,17}... | collective-permute-start | bytes 20 | tf_op jit(solution)/shard_map/ppermute | solution.py:41
  153.9 2.5 %collective-permute-done.8 = f32[1,1]{1,0:T(1,128)} collective-permute-done((f32[1,1]{1,0:T(1,128)}, f32[1,1]{1,0:T(1,128)}, u32[]{:S(2)}, u32[]{:S(2)}) %collective-permute-start.8) | collective-permute-done | bytes 36 | tf_op jit(solution)/shard_map/ppermute | solution.py:41
  157.1 5.8 %all-to-all-start.2 = ((bf16[4,34,6144]{2,1,0:T(8,128)(2,1)}), bf16[4,34,6144]{2,1,0:T(8,128)(2,1)}, u32[]{:S(2)}, u32[]{:S(2)}) async-start(bf16[4,34,6144]{2,1,0:T(8,128)(2,1)} %constant_dynamic-slice_fusion), calls=%async_computation.2 | async-start | bytes 3932160 | tf_op jit(solution)/shard_map/all_to_all | solution.py:33
  164.5 5.1 %collective-permute-start.2 = (bf16[136,1024]{1,0:T(8,128)(2,1)}, bf16[136,1024]{1,0:T(8,128)(2,1)}, u32[]{:S(2)}, u32[]{:S(2)}) collective-permute-start(bf16[136,1024]{1,0:T(8,128)(2,1)} %reshape.95), channel_id=1, source_target_pairs={{0,32},{8,40},{16,48},{24,56},{32,0},{40,8},{48,16},{56,24},{1,33}... | collective-permute-start | bytes 835592 | tf_op jit(solution)/shard_map/ppermute | solution.py:38
  171.2 2.4 %reshape.102 = bf16[136,3072]{1,0:T(8,128)(2,1)} reshape(bf16[4,34,3072]{2,1,0:T(8,128)(2,1)} %all-to-all-done.3) | data formatting | bytes 1671168 | tf_op jit(solution)/shard_map/reshape | solution.py:103
  175.4 9.9 %all-to-all-done.2 = bf16[4,34,6144]{2,1,0:T(8,128)(2,1)} async-done(((bf16[4,34,6144]{2,1,0:T(8,128)(2,1)}), bf16[4,34,6144]{2,1,0:T(8,128)(2,1)}, u32[]{:S(2)}, u32[]{:S(2)}) %all-to-all-start.2) | async-done | bytes 1671200 | tf_op jit(solution)/shard_map/all_to_all | solution.py:33
  185.2 3.2 %reshape.100 = bf16[136,6144]{1,0:T(8,128)(2,1)} reshape(bf16[4,34,6144]{2,1,0:T(8,128)(2,1)} %all-to-all-done.2) | data formatting | bytes 3342336 | tf_op jit(solution)/shard_map/reshape | solution.py:101
  188.5 2.6 %fusion.13 = f32[256]{0:T(256)S(1)} fusion(bf16[136,6144]{1,0:T(8,128)(2,1)} %reshape.100, bf16[128,6144]{1,0:T(8,128)(2,1)S(1)} %get-tuple-element.54, bf16[128,6144]{1,0:T(8,128)(2,1)S(1)} %get-tuple-element.55, s32[256]{0:T(256)S(1)} %copy-done.5), kind=kOutput, calls=%fused_computation.25 | convolution fusion | flops 434214656 | bytes 4818944 | tf_op jit(solution)/shard_map/dot_general | solution.py:136
  191.1 5.9 %collective-permute-done.2 = bf16[136,1024]{1,0:T(8,128)(2,1)} collective-permute-done((bf16[136,1024]{1,0:T(8,128)(2,1)}, bf16[136,1024]{1,0:T(8,128)(2,1)}, u32[]{:S(2)}, u32[]{:S(2)}) %collective-permute-start.2) | collective-permute-done | bytes 278560 | tf_op jit(solution)/shard_map/ppermute | solution.py:38
  (52 shorter events, 31.5 us)
Async XLA Ops:
  3.5 79.7 %collective-permute-start = (bf16[136,1536]{1,0:T(8,128)(2,1)}, bf16[136,1536]{1,0:T(8,128)(2,1)}, u32[]{:S(2)}, u32[]{:S(2)}) collective-permute-start(bf16[136,1536]{1,0:T(8,128)(2,1)} %reshape.97), channel_id=1, source_target_pairs={{0,32},{8,40},{16,48},{24,56},{32,0},{40,8},{48,16},{56,24},{1,33}... | collective-permute-start | bytes 1253384 | tf_op jit(solution)/shard_map/ppermute | solution.py:38
  19.3 7.7 %copy-start = (f32[1,2,6144]{2,1,0:T(2,128)S(1)}, f32[1,2,6144]{2,1,0:T(2,128)}, u32[]{:S(2)}) copy-start(f32[1,2,6144]{2,1,0:T(2,128)} %param.14) | copy-start | bytes 147460
  19.3 7.7 %copy-start.1 = (f32[2,6144]{1,0:T(2,128)S(1)}, f32[2,6144]{1,0:T(2,128)}, u32[]{:S(2)}) copy-start(f32[2,6144]{1,0:T(2,128)} %param.13) | copy-start | bytes 147460
  19.3 81.5 %collective-permute-start.3 = (bf16[136,1536]{1,0:T(8,128)(2,1)}, bf16[136,1536]{1,0:T(8,128)(2,1)}, u32[]{:S(2)}, u32[]{:S(2)}) collective-permute-start(bf16[136,1536]{1,0:T(8,128)(2,1)} %reshape.99), channel_id=1, source_target_pairs={{0,32},{8,40},{16,48},{24,56},{32,0},{40,8},{48,16},{56,24},{1,33}... | collective-permute-start | bytes 1253384 | tf_op jit(solution)/shard_map/ppermute | solution.py:38
  27.0 36.4 %copy-start.4 = (f32[128,2]{0,1:T(2,128)S(1)}, f32[128,2]{0,1:T(2,128)}, u32[]{:S(2)}) copy-start(f32[128,2]{0,1:T(2,128)} %param.11) | copy-start | bytes 3076
  56.6 10.4 %all-to-all-start.1 = ((bf16[4,34,1024]{2,1,0:T(8,128)(2,1)}), bf16[4,34,1024]{2,1,0:T(8,128)(2,1)S(1)}, u32[]{:S(2)}, u32[]{:S(2)}) async-start(bf16[4,34,1024]{2,1,0:T(8,128)(2,1)} %constant_dynamic-slice_fusion.3), calls=%async_computation.1 | async-start | bytes 655360 | tf_op jit(solution)/shard_map/all_to_all | solution.py:33
  63.4 2.2 %copy-start.3 = (s32[128,2]{0,1:T(2,128)S(1)}, s32[128,2]{0,1:T(2,128)}, u32[]{:S(2)}) copy-start(s32[128,2]{0,1:T(2,128)} %param.12) | copy-start | bytes 3076
  67.0 30.2 %all-to-all-start = ((bf16[4,34,2048]{2,1,0:T(8,128)(2,1)}), bf16[4,34,2048]{2,1,0:T(8,128)(2,1)}, u32[]{:S(2)}, u32[]{:S(2)}) async-start(bf16[4,34,2048]{2,1,0:T(8,128)(2,1)} %constant_dynamic-slice_fusion.4), calls=%async_computation | async-start | bytes 1310720 | tf_op jit(solution)/shard_map/all_to_all | solution.py:33
  83.2 33.0 %collective-permute-start.4 = (f32[1,1]{1,0:T(1,128)}, f32[1,1]{1,0:T(1,128)}, u32[]{:S(2)}, u32[]{:S(2)}) collective-permute-start(f32[1,1]{1,0:T(1,128)} %bitcast.2), channel_id=1, source_target_pairs={{0,0},{8,8},{16,16},{24,24},{1,1},{9,9},{17,17},{25,25},{2,2},{10,... | collective-permute-start | bytes 20 | tf_op jit(solution)/shard_map/ppermute | solution.py:49
  85.0 31.3 %collective-permute-start.5 = (f32[1,1]{1,0:T(1,128)}, f32[1,1]{1,0:T(1,128)}, u32[]{:S(2)}, u32[]{:S(2)}) collective-permute-start(f32[1,1]{1,0:T(1,128)} %bitcast.2), channel_id=1, source_target_pairs={{0,32},{8,40},{16,48},{24,56},{1,33},{9,41},{17,49},{25,57},{2,34}... | collective-permute-start | bytes 20 | tf_op jit(solution)/shard_map/ppermute | solution.py:49
  100.8 63.6 %collective-permute-start.1 = (bf16[136,1024]{1,0:T(8,128)(2,1)}, bf16[136,1024]{1,0:T(8,128)(2,1)}, u32[]{:S(2)}, u32[]{:S(2)}) collective-permute-start(bf16[136,1024]{1,0:T(8,128)(2,1)} %reshape.96), channel_id=1, source_target_pairs={{0,32},{8,40},{16,48},{24,56},{32,0},{40,8},{48,16},{56,24},{1,33}... | collective-permute-start | bytes 835592 | tf_op jit(solution)/shard_map/ppermute | solution.py:38
  104.2 66.6 %collective-permute-start.6 = (bf16[136,1024]{1,0:T(8,128)(2,1)}, bf16[136,1024]{1,0:T(8,128)(2,1)S(1)}, u32[]{:S(2)}, u32[]{:S(2)}) collective-permute-start(bf16[136,1024]{1,0:T(8,128)(2,1)} %reshape.98), channel_id=1, source_target_pairs={{0,32},{8,40},{16,48},{24,56},{32,0},{40,8},{48,16},{56,24},{1,33}... | collective-permute-start | bytes 835592 | tf_op jit(solution)/shard_map/ppermute | solution.py:38
  131.2 15.6 %collective-permute-start.7 = (f32[1,1]{1,0:T(1,128)}, f32[1,1]{1,0:T(1,128)}, u32[]{:S(2)}, u32[]{:S(2)}) collective-permute-start(f32[1,1]{1,0:T(1,128)} %psum.15), channel_id=1, source_target_pairs={{0,8},{8,0},{16,24},{24,16},{32,40},{40,32},{48,56},{56,48},{1,9},... | collective-permute-start | bytes 20 | tf_op jit(solution)/shard_map/ppermute | solution.py:41
  138.1 19.0 %all-to-all-start.3 = ((bf16[4,34,3072]{2,1,0:T(8,128)(2,1)}), bf16[4,34,3072]{2,1,0:T(8,128)(2,1)}, u32[]{:S(2)}, u32[]{:S(2)}) async-start(bf16[4,34,3072]{2,1,0:T(8,128)(2,1)} %reshape.101), calls=%async_computation.3 | async-start | bytes 1966080 | tf_op jit(solution)/shard_map/all_to_all | solution.py:33
  148.0 8.5 %collective-permute-start.8 = (f32[1,1]{1,0:T(1,128)}, f32[1,1]{1,0:T(1,128)}, u32[]{:S(2)}, u32[]{:S(2)}) collective-permute-start(f32[1,1]{1,0:T(1,128)} %add.87), channel_id=1, source_target_pairs={{0,16},{8,24},{16,0},{24,8},{32,48},{40,56},{48,32},{56,40},{1,17}... | collective-permute-start | bytes 20 | tf_op jit(solution)/shard_map/ppermute | solution.py:41
  157.1 5.9 %copy-start.2 = (f32[2,6144]{1,0:T(2,128)S(1)}, f32[2,6144]{1,0:T(2,128)}, u32[]{:S(2)}) copy-start(f32[2,6144]{1,0:T(2,128)} %param.13) | copy-start | bytes 147460
  157.1 28.1 %all-to-all-start.2 = ((bf16[4,34,6144]{2,1,0:T(8,128)(2,1)}), bf16[4,34,6144]{2,1,0:T(8,128)(2,1)}, u32[]{:S(2)}, u32[]{:S(2)}) async-start(bf16[4,34,6144]{2,1,0:T(8,128)(2,1)} %constant_dynamic-slice_fusion), calls=%async_computation.2 | async-start | bytes 3932160 | tf_op jit(solution)/shard_map/all_to_all | solution.py:33
  164.5 32.5 %collective-permute-start.2 = (bf16[136,1024]{1,0:T(8,128)(2,1)}, bf16[136,1024]{1,0:T(8,128)(2,1)}, u32[]{:S(2)}, u32[]{:S(2)}) collective-permute-start(bf16[136,1024]{1,0:T(8,128)(2,1)} %reshape.95), channel_id=1, source_target_pairs={{0,32},{8,40},{16,48},{24,56},{32,0},{40,8},{48,16},{56,24},{1,33}... | collective-permute-start | bytes 835592 | tf_op jit(solution)/shard_map/ppermute | solution.py:38
  175.3 13.1 %copy-start.5 = (s32[256]{0:T(256)S(1)}, s32[256]{0:T(256)}, u32[]{:S(2)}) copy-start(s32[256]{0:T(256)} %get-tuple-element.60) | copy-start | bytes 3076

commit v3 on v2

--- a/solution.py
+++ b/solution.py
@@ -3,9 +3,7 @@
 from jax import lax
 from jax.sharding import PartitionSpec as P
 
-CUTS = (0, 1536, 3072, 4096, 5120, 6144)
-EARLY = 2
-FLIGHT = 2
+HEAD = 1536
 AXES = ("replica", "expert", "fsdp")
 
 
@@ -45,64 +43,53 @@
 
     depth = 2 * runs
 
-    def along_z(value, start):
+    def along_z(value):
         return lax.ppermute(
             value,
             AXES,
             [
-                (place(r, z, x), place(r, (z + start + r) % depth, x))
+                (place(r, z, x), place(r, (z + r + x // 2 * replicas) % depth, x))
                 for r in range(replicas)
                 for z in range(depth)
                 for x in range(side)
             ],
         )
 
+    def tie(*values):
+        return lax.optimization_barrier(values)
+
     saved = saved_out.reshape(owners, capacity, width)
     other = 1 - half
 
-    def part(which, first, last, rows=saved):
+    def part(which, first, last):
         return lax.dynamic_slice(
-            rows, (which * side, 0, first), (side, capacity, last - first)
+            saved, (which * side, 0, first), (side, capacity, last - first)
         )
 
-    pseudo = (
-        lax.psum((outer_params - local_params[0]).astype(jnp.bfloat16), "replica").astype(
-            jnp.float32
-        )
-        / replicas
-    )
+    crossed = over_z(part(other, 0, HEAD).reshape(block, HEAD))
+    spread = along_x(part(other, HEAD, width)).reshape(block, width - HEAD)
+
+    def over_replicas(value):
+        every = jnp.broadcast_to(value[None], (replicas, *value.shape))
+        every = lax.all_to_all(every, "replica", split_axis=0, concat_axis=0, tiled=True)
+        return jnp.sum(every.astype(jnp.float32), axis=0)
+
+    pseudo = over_replicas((outer_params - local_params[0]).astype(jnp.bfloat16)) / replicas
     own_sq = jnp.sum(pseudo * pseudo).reshape(1, 1)
-    after_sum, own_sq = lax.optimization_barrier((saved, own_sq))
 
-    pieces = len(CUTS) - 1
-    middle = EARLY + 1
-    spread = {}
-    for first, last in ((EARLY, middle), (middle, pieces)):
-        rows = along_x(part(other, CUTS[first], CUTS[last], after_sum))
-        for i in range(first, last):
-            spread[i] = rows[:, :, CUTS[i] - CUTS[first] : CUTS[i + 1] - CUTS[first]]
-    came = []
-    for i in range(pieces):
-        rows = part(other, CUTS[i], CUTS[i + 1]) if i < EARLY else spread[i]
-        rows = rows.reshape(block, CUTS[i + 1] - CUTS[i])
-        if i >= FLIGHT:
-            rows, came[i - FLIGHT] = lax.optimization_barrier((rows, came[i - FLIGHT]))
-        came.append(over_z(rows))
-        if i == 0:
-            came[0], own_sq = lax.optimization_barrier((came[0], own_sq))
-            window = along_z(own_sq, 0) + along_z(own_sq, replicas)
-
-    after_early, came[1], window = lax.optimization_barrier((after_sum, came[1], window))
-    window = lax.psum(window, "replica")
-    window = window + swap_x(window, 1)
-    total_sq = (window + swap_x(window, 2))[0, 0]
-
-    near = lax.dynamic_slice_in_dim(after_early, half * side, side, 0)
+    own_sq = own_sq + swap_x(own_sq, 2)
+    window = along_z(own_sq)
+    crossed, spread, window = tie(crossed, spread, window)
+    came = over_z(spread)
+    window = over_replicas(window)
+    crossed, window, half_then, top_logits = tie(crossed, window, half, top_logits)
+    window = window + swap_x(window, 2)
+    total_sq = (window + swap_x(window, 1))[0, 0]
+    near = lax.dynamic_slice_in_dim(saved, half_then * side, side, 0)
     near_rows = along_x(near).reshape(block, width)
-    crossed = jnp.concatenate(came[:EARLY], axis=1).reshape(side, capacity, CUTS[EARLY])
-    crossed = along_x(crossed).reshape(block, CUTS[EARLY])
-    far_rows = [crossed] + came[EARLY:]
-    cuts = (0,) + CUTS[EARLY:]
+    crossed = along_x(crossed.reshape(side, capacity, HEAD)).reshape(block, HEAD)
+    far_rows = [crossed, came]
+    cuts = (0, HEAD, width)
 
     count = jnp.arange(owners, dtype=jnp.int32)
     named = [(expert_ids[:, k : k + 1] == count[None, :]).astype(jnp.bfloat16) for k in range(2)]

time: 200 us -> 192 us (0.960)
  the two profiles are of different devices: /device:TPU:34 before, /device:TPU:59 now
where the time goes in v3:
time: 192 us; the launch traced here: 191 us
  waiting for transfers between devices  79.3 us (41%)
  starting transfers between devices  59.1 us (31%)
  local copies, waits for them, and re-layouts  21.5 us (11%)
  blocking collectives  8.99 us (5%)
  other arithmetic  8.93 us (5%)
  matrix products  7.77 us (4%)
  between operations  5.53 us (3%)
    ppermute x2, waiting for transfers between devices, over_z(): return lax.ppermute(value, 'expert', across)  48.1 us
    ppermute x2, starting transfers between devices, over_z(): return lax.ppermute(value, 'expert', across)  26.5 us
    all_to_all x3, waiting for transfers between devices, along_x(): lax.all_to_all(value, 'expert', split_axis=0, concat_axis=0, axis_index_g...  16.7 us
    all_to_all x3, starting transfers between devices, along_x(): lax.all_to_all(value, 'expert', split_axis=0, concat_axis=0, axis_index_g...  13.4 us
    ppermute x3, starting transfers between devices, swap_x(): return lax.ppermute(value, 'expert', [(e, e ^ step) for e in range(owners)])  10 us
    all_to_all x1, blocking collectives, over_replicas(): lax.all_to_all(every, 'replica', split_axis=0, concat_axis=0, tiled=True)  8.99 us
    dot_general x3, matrix products, inner(): lax.dot_general(a, b, (((1,), (1,)), ((), ())), preferred_element_type=jn...  7.62 us
    ppermute x3, waiting for transfers between devices, swap_x(): return lax.ppermute(value, 'expert', [(e, e ^ step) for e in range(owners)])  6.84 us
  transfers between devices with their start and end apart: 10, of which 8 were waited for; matrix products, arithmetic and copies ran while one was open for 17% of the time, Pallas kernels for 0%

profile of v3, /device:TPU:59, one launch (start us, length us, event | category | flops | bytes accessed | tf_op | source)
XLA Modules:
  0.0 191.2 jit_solution(6970121924334205252)
XLA Ops:
  2.4 5.0 %all-to-all-start.1 = ((bf16[8,2,6144]{2,1,0:T(2,128)(2,1)}), bf16[8,2,6144]{2,1,0:T(2,128)(2,1)S(1)}, u32[]{:S(2)}, u32[]{:S(2)}) async-start(bf16[8,2,6144]{2,1,0:T(2,128)(2,1)} %broadcast_in_dim.16), calls=%async_computation.1 | async-start | bytes 393216 | tf_op jit(solution)/shard_map/all_to_all | solution.py:74
  9.4 2.2 %all-to-all-done.1 = bf16[8,2,6144]{2,1,0:T(2,128)(2,1)S(1)} async-done(((bf16[8,2,6144]{2,1,0:T(2,128)(2,1)}), bf16[8,2,6144]{2,1,0:T(2,128)(2,1)S(1)}, u32[]{:S(2)}, u32[]{:S(2)}) %all-to-all-start.1) | async-done | bytes 196640 | tf_op jit(solution)/shard_map/all_to_all | solution.py:74
  11.6 4.5 %all-to-all-start = ((bf16[4,34,4608]{2,1,0:T(8,128)(2,1)}), bf16[4,34,4608]{2,1,0:T(8,128)(2,1)}, u32[]{:S(2)}, u32[]{:S(2)}) async-start(bf16[4,34,4608]{2,1,0:T(8,128)(2,1)} %copy.29), calls=%async_computation | async-start | bytes 2949120 | tf_op jit(solution)/shard_map/all_to_all | solution.py:31
  19.1 14.5 %collective-permute-start = (bf16[136,1536]{1,0:T(8,128)(2,1)}, bf16[136,1536]{1,0:T(8,128)(2,1)}, u32[]{:S(2)}, u32[]{:S(2)}) collective-permute-start(bf16[136,1536]{1,0:T(8,128)(2,1)} %reshape.87), channel_id=1, source_target_pairs={{0,32},{8,40},{16,48},{24,56},{32,0},{40,8},{48,16},{56,24},{1,33}... | collective-permute-start | bytes 1253384 | tf_op jit(solution)/shard_map/ppermute | solution.py:36
  38.5 3.7 %collective-permute-start.1 = (f32[1,1]{1,0:T(1,128)}, f32[1,1]{1,0:T(1,128)}, u32[]{:S(2)}, u32[]{:S(2)}) collective-permute-start(f32[1,1]{1,0:T(1,128)} %bitcast.2), channel_id=1, source_target_pairs={{0,16},{8,24},{16,0},{24,8},{32,48},{40,56},{48,32},{56,40},{1,17}... | collective-permute-start | bytes 20 | tf_op jit(solution)/shard_map/ppermute | solution.py:39
  42.2 2.2 %collective-permute-done.1 = f32[1,1]{1,0:T(1,128)} collective-permute-done((f32[1,1]{1,0:T(1,128)}, f32[1,1]{1,0:T(1,128)}, u32[]{:S(2)}, u32[]{:S(2)}) %collective-permute-start.1) | collective-permute-done | bytes 36 | tf_op jit(solution)/shard_map/ppermute | solution.py:39
  45.6 4.3 %collective-permute-start.2 = (f32[1,1]{1,0:T(1,128)}, f32[1,1]{1,0:T(1,128)}, u32[]{:S(2)}, u32[]{:S(2)}) collective-permute-start(f32[1,1]{1,0:T(1,128)} %add.63), channel_id=1, source_target_pairs={{0,0},{8,8},{16,48},{24,56},{1,1},{9,9},{17,49},{25,57},{2,2},{10,... | collective-permute-start | bytes 20 | tf_op jit(solution)/shard_map/ppermute | solution.py:47
  49.9 2.8 %reshape.88 = bf16[136,4608]{1,0:T(8,128)(2,1)} reshape(bf16[4,34,4608]{2,1,0:T(8,128)(2,1)} %all-to-all-done) | data formatting | bytes 2506752 | tf_op jit(solution)/shard_map/reshape | solution.py:70
  52.7 5.5 %collective-permute-done.2 = f32[1,1]{1,0:T(1,128)} collective-permute-done((f32[1,1]{1,0:T(1,128)}, f32[1,1]{1,0:T(1,128)}, u32[]{:S(2)}, u32[]{:S(2)}) %collective-permute-start.2) | collective-permute-done | bytes 36 | tf_op jit(solution)/shard_map/ppermute | solution.py:47
  58.2 11.9 %collective-permute-done = bf16[136,1536]{1,0:T(8,128)(2,1)} collective-permute-done((bf16[136,1536]{1,0:T(8,128)(2,1)}, bf16[136,1536]{1,0:T(8,128)(2,1)}, u32[]{:S(2)}, u32[]{:S(2)}) %collective-permute-start) | collective-permute-done | bytes 417824 | tf_op jit(solution)/shard_map/ppermute | solution.py:36
  70.0 11.9 %collective-permute-start.3 = (bf16[136,4608]{1,0:T(8,128)(2,1)}, bf16[136,4608]{1,0:T(8,128)(2,1)}, u32[]{:S(2)}, u32[]{:S(2)}) collective-permute-start(bf16[136,4608]{1,0:T(8,128)(2,1)} %reshape.88), channel_id=1, source_target_pairs={{0,32},{8,40},{16,48},{24,56},{32,0},{40,8},{48,16},{56,24},{1,33}... | collective-permute-start | bytes 3760136 | tf_op jit(solution)/shard_map/ppermute | solution.py:36
  82.6 9.0 %all_to_all.25 = f32[8,1,1]{2,1,0:T(1,128)S(1)} all-to-all(f32[8,1,1]{2,1,0:T(1,128)S(1)} %broadcast_in_dim.20), channel_id=1, replica_groups=mesh['replica'=8,'expert'=8,'fsdp'=8] {'replica'}, dimensions={0} | all-to-all | bytes 64 | tf_op jit(solution)/shard_map/all_to_all | solution.py:74
  94.9 4.3 %all-to-all-start.4 = ((bf16[4,34,1536]{2,1,0:T(8,128)(2,1)}), bf16[4,34,1536]{2,1,0:T(8,128)(2,1)}, u32[]{:S(2)}, u32[]{:S(2)}) async-start(bf16[4,34,1536]{2,1,0:T(8,128)(2,1)} %reshape.91), calls=%async_computation.4 | async-start | bytes 983040 | tf_op jit(solution)/shard_map/all_to_all | solution.py:31
  99.2 3.8 %fusion = (bf16[128,6144]{1,0:T(8,128)(2,1)}, bf16[128,6144]{1,0:T(8,128)(2,1)}) fusion(bf16[128,6144]{1,0:T(8,128)(2,1)} %param.9, f32[128]{0:T(128)S(1)} %bitcast.52, f32[128]{0:T(128)S(1)} %get-tuple-element.38), kind=kLoop, calls=%fused_computation.2 | loop fusion | flops 3932160 | bytes 4719616 | tf_op jit(solution)/shard_map/convert_element_type | solution.py:117
  104.0 2.2 %copy.32 = bf16[4,34,6144]{2,1,0:T(8,128)(2,1)} copy(bf16[4,34,6144]{2,0,1:T(4,128)(2,1)S(1)} %dynamic-slice_bitcast_fusion) | data formatting | bytes 3342336 | tf_op jit(solution)/shard_map/dynamic_slice | solution.py:88
  106.3 3.7 %collective-permute-start.4 = (f32[1,1]{1,0:T(1,128)}, f32[1,1]{1,0:T(1,128)}, u32[]{:S(2)}, u32[]{:S(2)}) collective-permute-start(f32[1,1]{1,0:T(1,128)} %bitcast.10), channel_id=1, source_target_pairs={{0,16},{8,24},{16,0},{24,8},{32,48},{40,56},{48,32},{56,40},{1,17}... | collective-permute-start | bytes 20 | tf_op jit(solution)/shard_map/ppermute | solution.py:39
  110.0 2.6 %collective-permute-done.4 = f32[1,1]{1,0:T(1,128)} collective-permute-done((f32[1,1]{1,0:T(1,128)}, f32[1,1]{1,0:T(1,128)}, u32[]{:S(2)}, u32[]{:S(2)}) %collective-permute-start.4) | collective-permute-done | bytes 36 | tf_op jit(solution)/shard_map/ppermute | solution.py:39
  113.9 2.6 %collective-permute-start.5 = (f32[1,1]{1,0:T(1,128)}, f32[1,1]{1,0:T(1,128)}, u32[]{:S(2)}, u32[]{:S(2)}) collective-permute-start(f32[1,1]{1,0:T(1,128)} %add.73), channel_id=1, source_target_pairs={{0,8},{8,0},{16,24},{24,16},{32,40},{40,32},{48,56},{56,48},{1,9},... | collective-permute-start | bytes 20 | tf_op jit(solution)/shard_map/ppermute | solution.py:39
  119.4 4.6 %all-to-all-start.3 = ((bf16[4,34,6144]{2,1,0:T(8,128)(2,1)}), bf16[4,34,6144]{2,1,0:T(8,128)(2,1)}, u32[]{:S(2)}, u32[]{:S(2)}) async-start(bf16[4,34,6144]{2,1,0:T(8,128)(2,1)} %copy.32), calls=%async_computation.3 | async-start | bytes 3932160 | tf_op jit(solution)/shard_map/all_to_all | solution.py:31
  128.3 16.7 %all-to-all-done.3 = bf16[4,34,6144]{2,1,0:T(8,128)(2,1)} async-done(((bf16[4,34,6144]{2,1,0:T(8,128)(2,1)}), bf16[4,34,6144]{2,1,0:T(8,128)(2,1)}, u32[]{:S(2)}, u32[]{:S(2)}) %all-to-all-start.3) | async-done | bytes 1671200 | tf_op jit(solution)/shard_map/all_to_all | solution.py:31
  145.0 3.3 %reshape.90 = bf16[136,6144]{1,0:T(8,128)(2,1)} reshape(bf16[4,34,6144]{2,1,0:T(8,128)(2,1)} %all-to-all-done.3) | data formatting | bytes 3342336 | tf_op jit(solution)/shard_map/reshape | solution.py:89
  148.3 3.7 %fusion.17 = f32[256]{0:T(256)S(1)} fusion(bf16[136,6144]{1,0:T(8,128)(2,1)} %reshape.90, bf16[128,6144]{1,0:T(8,128)(2,1)} %get-tuple-element.41, bf16[128,6144]{1,0:T(8,128)(2,1)} %get-tuple-element.40, s32[256]{0:T(256)S(1)} %copy-done.9), kind=kOutput, calls=%fused_computation.18 | convolution fusion | flops 434214656 | bytes 4818944 | tf_op jit(solution)/shard_map/dot_general | solution.py:123
  152.1 36.3 %collective-permute-done.3 = bf16[136,4608]{1,0:T(8,128)(2,1)} collective-permute-done((bf16[136,4608]{1,0:T(8,128)(2,1)}, bf16[136,4608]{1,0:T(8,128)(2,1)}, u32[]{:S(2)}, u32[]{:S(2)}) %collective-permute-start.3) | collective-permute-done | bytes 1253408 | tf_op jit(solution)/shard_map/ppermute | solution.py:36
  188.3 2.2 %fusion.20 = f32[256]{0:T(256)S(1)} fusion(bf16[136,4608]{1,0:T(8,128)(2,1)} %collective-permute-done.3, bf16[128,6144]{1,0:T(8,128)(2,1)S(1)} %copy-done.2, bf16[128,6144]{1,0:T(8,128)(2,1)S(1)} %copy-done.1, s32[256]{0:T(256)S(1)} %get-tuple-element.44), kind=kOutput, calls=%fused_computation.19 | convolution fusion | flops 325687040 | bytes 4401152 | tf_op jit(solution)/shard_map/dot_general | solution.py:123
  (49 shorter events, 22.1 us)
Async XLA Ops:
  0.6 6.8 %copy-start = (bf16[1,1,1,8,34,6144]{5,3,4,2,1,0:T(8,128)(2,1)S(1)}, bf16[1,1,1,8,34,6144]{5,3,4,2,1,0:T(8,128)(2,1)}, u32[]{:S(2)}) copy-start(bf16[1,1,1,8,34,6144]{5,3,4,2,1,0:T(8,128)(2,1)} %param.10) | copy-start | bytes 10027012
  2.4 9.2 %all-to-all-start.1 = ((bf16[8,2,6144]{2,1,0:T(2,128)(2,1)}), bf16[8,2,6144]{2,1,0:T(2,128)(2,1)S(1)}, u32[]{:S(2)}, u32[]{:S(2)}) async-start(bf16[8,2,6144]{2,1,0:T(2,128)(2,1)} %broadcast_in_dim.16), calls=%async_computation.1 | async-start | bytes 393216 | tf_op jit(solution)/shard_map/all_to_all | solution.py:74
  11.6 38.3 %all-to-all-start = ((bf16[4,34,4608]{2,1,0:T(8,128)(2,1)}), bf16[4,34,4608]{2,1,0:T(8,128)(2,1)}, u32[]{:S(2)}, u32[]{:S(2)}) async-start(bf16[4,34,4608]{2,1,0:T(8,128)(2,1)} %copy.29), calls=%async_computation | async-start | bytes 2949120 | tf_op jit(solution)/shard_map/all_to_all | solution.py:31
  16.1 17.5 %copy-start.8 = (s32[128,2]{0,1:T(2,128)S(1)}, s32[128,2]{0,1:T(2,128)}, u32[]{:S(2)}) copy-start(s32[128,2]{0,1:T(2,128)} %param.12) | copy-start | bytes 3076
  19.1 50.9 %collective-permute-start = (bf16[136,1536]{1,0:T(8,128)(2,1)}, bf16[136,1536]{1,0:T(8,128)(2,1)}, u32[]{:S(2)}, u32[]{:S(2)}) collective-permute-start(bf16[136,1536]{1,0:T(8,128)(2,1)} %reshape.87), channel_id=1, source_target_pairs={{0,32},{8,40},{16,48},{24,56},{32,0},{40,8},{48,16},{56,24},{1,33}... | collective-permute-start | bytes 1253384 | tf_op jit(solution)/shard_map/ppermute | solution.py:36
  37.2 0.6 copy-start.3
  38.5 5.9 %collective-permute-start.1 = (f32[1,1]{1,0:T(1,128)}, f32[1,1]{1,0:T(1,128)}, u32[]{:S(2)}, u32[]{:S(2)}) collective-permute-start(f32[1,1]{1,0:T(1,128)} %bitcast.2), channel_id=1, source_target_pairs={{0,16},{8,24},{16,0},{24,8},{32,48},{40,56},{48,32},{56,40},{1,17}... | collective-permute-start | bytes 20 | tf_op jit(solution)/shard_map/ppermute | solution.py:39
  45.6 12.6 %collective-permute-start.2 = (f32[1,1]{1,0:T(1,128)}, f32[1,1]{1,0:T(1,128)}, u32[]{:S(2)}, u32[]{:S(2)}) collective-permute-start(f32[1,1]{1,0:T(1,128)} %add.63), channel_id=1, source_target_pairs={{0,0},{8,8},{16,48},{24,56},{1,1},{9,9},{17,49},{25,57},{2,2},{10,... | collective-permute-start | bytes 20 | tf_op jit(solution)/shard_map/ppermute | solution.py:47
  70.0 118.3 %collective-permute-start.3 = (bf16[136,4608]{1,0:T(8,128)(2,1)}, bf16[136,4608]{1,0:T(8,128)(2,1)}, u32[]{:S(2)}, u32[]{:S(2)}) collective-permute-start(bf16[136,4608]{1,0:T(8,128)(2,1)} %reshape.88), channel_id=1, source_target_pairs={{0,32},{8,40},{16,48},{24,56},{32,0},{40,8},{48,16},{56,24},{1,33}... | collective-permute-start | bytes 3760136 | tf_op jit(solution)/shard_map/ppermute | solution.py:36
  94.9 24.5 %all-to-all-start.4 = ((bf16[4,34,1536]{2,1,0:T(8,128)(2,1)}), bf16[4,34,1536]{2,1,0:T(8,128)(2,1)}, u32[]{:S(2)}, u32[]{:S(2)}) async-start(bf16[4,34,1536]{2,1,0:T(8,128)(2,1)} %reshape.91), calls=%async_computation.4 | async-start | bytes 983040 | tf_op jit(solution)/shard_map/all_to_all | solution.py:31
  106.3 6.3 %collective-permute-start.4 = (f32[1,1]{1,0:T(1,128)}, f32[1,1]{1,0:T(1,128)}, u32[]{:S(2)}, u32[]{:S(2)}) collective-permute-start(f32[1,1]{1,0:T(1,128)} %bitcast.10), channel_id=1, source_target_pairs={{0,16},{8,24},{16,0},{24,8},{32,48},{40,56},{48,32},{56,40},{1,17}... | collective-permute-start | bytes 20 | tf_op jit(solution)/shard_map/ppermute | solution.py:39
  113.9 4.7 %collective-permute-start.5 = (f32[1,1]{1,0:T(1,128)}, f32[1,1]{1,0:T(1,128)}, u32[]{:S(2)}, u32[]{:S(2)}) collective-permute-start(f32[1,1]{1,0:T(1,128)} %add.73), channel_id=1, source_target_pairs={{0,8},{8,0},{16,24},{24,16},{32,40},{40,32},{48,56},{56,48},{1,9},... | collective-permute-start | bytes 20 | tf_op jit(solution)/shard_map/ppermute | solution.py:39
  119.4 4.6 %copy-start.4 = (f32[2,6144]{1,0:T(2,128)S(1)}, f32[2,6144]{1,0:T(2,128)}, u32[]{:S(2)}) copy-start(f32[2,6144]{1,0:T(2,128)} %copy-done.3) | copy-start | bytes 147460
  119.4 4.6 %copy-start.5 = (f32[1,2,6144]{2,1,0:T(2,128)S(1)}, f32[1,2,6144]{2,1,0:T(2,128)}, u32[]{:S(2)}) copy-start(f32[1,2,6144]{2,1,0:T(2,128)} %param.14) | copy-start | bytes 147460
  119.4 4.6 %copy-start.6 = (f32[2,6144]{1,0:T(2,128)S(1)}, f32[2,6144]{1,0:T(2,128)}, u32[]{:S(2)}) copy-start(f32[2,6144]{1,0:T(2,128)} %param.13) | copy-start | bytes 147460
  119.4 4.6 %copy-start.7 = (f32[2,6144]{1,0:T(2,128)S(1)}, f32[2,6144]{1,0:T(2,128)}, u32[]{:S(2)}) copy-start(f32[2,6144]{1,0:T(2,128)} %param.15) | copy-start | bytes 147460
  119.4 25.6 %all-to-all-start.3 = ((bf16[4,34,6144]{2,1,0:T(8,128)(2,1)}), bf16[4,34,6144]{2,1,0:T(8,128)(2,1)}, u32[]{:S(2)}, u32[]{:S(2)}) async-start(bf16[4,34,6144]{2,1,0:T(8,128)(2,1)} %copy.32), calls=%async_computation.3 | async-start | bytes 3932160 | tf_op jit(solution)/shard_map/all_to_all | solution.py:31
  128.3 20.0 %copy-start.9 = (s32[256]{0:T(256)S(1)}, s32[256]{0:T(256)}, u32[]{:S(2)}) copy-start(s32[256]{0:T(256)} %get-tuple-element.45) | copy-start | bytes 3076
  148.3 40.0 %copy-start.1 = (bf16[128,6144]{1,0:T(8,128)(2,1)S(1)}, bf16[128,6144]{1,0:T(8,128)(2,1)}, u32[]{:S(2)}) copy-start(bf16[128,6144]{1,0:T(8,128)(2,1)} %get-tuple-element.40) | copy-start | bytes 4718596
  148.3 40.0 %copy-start.2 = (bf16[128,6144]{1,0:T(8,128)(2,1)S(1)}, bf16[128,6144]{1,0:T(8,128)(2,1)}, u32[]{:S(2)}) copy-start(bf16[128,6144]{1,0:T(8,128)(2,1)} %get-tuple-element.41) | copy-start | bytes 4718596

commit v4 on v3

--- a/solution.py
+++ b/solution.py
@@ -3,7 +3,7 @@
 from jax import lax
 from jax.sharding import PartitionSpec as P
 
-HEAD = 1536
+HEAD = 2048
 AXES = ("replica", "expert", "fsdp")
 
 
@@ -74,7 +74,12 @@
         every = lax.all_to_all(every, "replica", split_axis=0, concat_axis=0, tiled=True)
         return jnp.sum(every.astype(jnp.float32), axis=0)
 
-    pseudo = over_replicas((outer_params - local_params[0]).astype(jnp.bfloat16)) / replicas
+    pseudo = (
+        lax.psum((outer_params - local_params[0]).astype(jnp.bfloat16), "replica").astype(
+            jnp.float32
+        )
+        / replicas
+    )
     own_sq = jnp.sum(pseudo * pseudo).reshape(1, 1)
 
     own_sq = own_sq + swap_x(own_sq, 2)

time: 192 us -> 186 us (0.969)
  the two profiles are of different devices: /device:TPU:59 before, /device:TPU:57 now
where the time goes in v4:
time: 186 us; the launch traced here: 185 us
  waiting for transfers between devices  57.6 us (31%)
  starting transfers between devices  51.4 us (28%)
  blocking collectives  33.7 us (18%)
  local copies, waits for them, and re-layouts  22.5 us (12%)
  matrix products  7.88 us (4%)
  other arithmetic  6.45 us (3%)
  between operations  5.52 us (3%)
    ppermute x2, waiting for transfers between devices, over_z(): return lax.ppermute(value, 'expert', across)  30.4 us
    psum x1, blocking collectives, shards(): lax.psum((outer_params - local_params[0]).astype(jnp.bfloat16), 'replica')  24.5 us
    ppermute x2, starting transfers between devices, over_z(): return lax.ppermute(value, 'expert', across)  22.1 us
    all_to_all x3, waiting for transfers between devices, along_x(): lax.all_to_all(value, 'expert', split_axis=0, concat_axis=0, axis_index_g...  18.1 us
    ppermute x3, starting transfers between devices, swap_x(): return lax.ppermute(value, 'expert', [(e, e ^ step) for e in range(owners)])  13.6 us
    all_to_all x3, starting transfers between devices, along_x(): lax.all_to_all(value, 'expert', split_axis=0, concat_axis=0, axis_index_g...  13 us
    all_to_all x1, blocking collectives, over_replicas(): lax.all_to_all(every, 'replica', split_axis=0, concat_axis=0, tiled=True)  9.15 us
    dot_general x3, matrix products, inner(): lax.dot_general(a, b, (((1,), (1,)), ((), ())), preferred_element_type=jn...  7.73 us
  transfers between devices with their start and end apart: 9, of which 5 were waited for; matrix products, arithmetic and copies ran while one was open for 15% of the time, Pallas kernels for 0%

profile of v4, /device:TPU:57, one launch (start us, length us, event | category | flops | bytes accessed | tf_op | source)
XLA Modules:
  0.0 185.0 jit_solution(17241001028296807940)
XLA Ops:
  0.7 1.9 %copy-done = bf16[1,1,1,8,34,6144]{5,3,4,2,1,0:T(8,128)(2,1)S(1)} copy-done((bf16[1,1,1,8,34,6144]{5,3,4,2,1,0:T(8,128)(2,1)S(1)}, bf16[1,1,1,8,34,6144]{5,3,4,2,1,0:T(8,128)(2,1)}, u32[]{:S(2)}) %copy-start) | copy-done | bytes 3342360
  4.1 2.1 %reshape.86 = bf16[136,2048]{1,0:T(8,128)(2,1)} reshape(bf16[1,1,1,4,34,2048]{5,4,3,2,1,0:T(8,128)(2,1)} %copy.23) | data formatting | bytes 1114112 | tf_op jit(solution)/shard_map/reshape | solution.py:69
  6.1 14.5 %collective-permute-start = (bf16[136,2048]{1,0:T(8,128)(2,1)}, bf16[136,2048]{1,0:T(8,128)(2,1)}, u32[]{:S(2)}, u32[]{:S(2)}) collective-permute-start(bf16[136,2048]{1,0:T(8,128)(2,1)} %reshape.86), channel_id=1, source_target_pairs={{0,32},{8,40},{16,48},{24,56},{32,0},{40,8},{48,16},{56,24},{1,33}... | collective-permute-start | bytes 1671176 | tf_op jit(solution)/shard_map/ppermute | solution.py:36
  23.1 4.4 %all-to-all-start = ((bf16[4,34,4096]{2,1,0:T(8,128)(2,1)}), bf16[4,34,4096]{2,1,0:T(8,128)(2,1)}, u32[]{:S(2)}, u32[]{:S(2)}) async-start(bf16[4,34,4096]{2,1,0:T(8,128)(2,1)} %copy.24), calls=%async_computation | async-start | bytes 2621440 | tf_op jit(solution)/shard_map/all_to_all | solution.py:31
  27.6 24.5 %psum.7 = bf16[2,6144]{1,0:T(2,128)(2,1)S(1)} all-reduce(bf16[2,6144]{1,0:T(2,128)(2,1)S(1)} %fusion.35), channel_id=1, replica_groups=mesh['replica'=8,'expert'=8,'fsdp'=8] {'replica'}, use_global_device_ids=true, to_apply=%region_0.1 | all-reduce | flops 12288 | bytes 49152 | tf_op jit(solution)/shard_map/psum | solution.py:78
  52.8 4.8 %collective-permute-start.1 = (f32[1,1]{1,0:T(1,128)}, f32[1,1]{1,0:T(1,128)}, u32[]{:S(2)}, u32[]{:S(2)}) collective-permute-start(f32[1,1]{1,0:T(1,128)} %bitcast.2), channel_id=1, source_target_pairs={{0,16},{8,24},{16,0},{24,8},{32,48},{40,56},{48,32},{56,40},{1,17}... | collective-permute-start | bytes 20 | tf_op jit(solution)/shard_map/ppermute | solution.py:39
  61.1 2.6 %collective-permute-start.2 = (f32[1,1]{1,0:T(1,128)}, f32[1,1]{1,0:T(1,128)}, u32[]{:S(2)}, u32[]{:S(2)}) collective-permute-start(f32[1,1]{1,0:T(1,128)} %add.65), channel_id=1, source_target_pairs={{0,0},{8,8},{16,48},{24,56},{1,1},{9,9},{17,49},{25,57},{2,2},{10,... | collective-permute-start | bytes 20 | tf_op jit(solution)/shard_map/ppermute | solution.py:47
  63.7 2.6 %reshape.87 = bf16[136,4096]{1,0:T(8,128)(2,1)} reshape(bf16[4,34,4096]{2,1,0:T(8,128)(2,1)} %all-to-all-done) | data formatting | bytes 2228224 | tf_op jit(solution)/shard_map/reshape | solution.py:70
  66.3 7.0 %collective-permute-done.2 = f32[1,1]{1,0:T(1,128)} collective-permute-done((f32[1,1]{1,0:T(1,128)}, f32[1,1]{1,0:T(1,128)}, u32[]{:S(2)}, u32[]{:S(2)}) %collective-permute-start.2) | collective-permute-done | bytes 36 | tf_op jit(solution)/shard_map/ppermute | solution.py:47
  73.3 7.6 %collective-permute-start.3 = (bf16[136,4096]{1,0:T(8,128)(2,1)}, bf16[136,4096]{1,0:T(8,128)(2,1)}, u32[]{:S(2)}, u32[]{:S(2)}) collective-permute-start(bf16[136,4096]{1,0:T(8,128)(2,1)} %reshape.87), channel_id=1, source_target_pairs={{0,32},{8,40},{16,48},{24,56},{32,0},{40,8},{48,16},{56,24},{1,33}... | collective-permute-start | bytes 3342344 | tf_op jit(solution)/shard_map/ppermute | solution.py:36
  81.6 9.1 %all_to_all.20 = f32[8,1,1]{2,1,0:T(1,128)S(1)} all-to-all(f32[8,1,1]{2,1,0:T(1,128)S(1)} %broadcast_in_dim.30), channel_id=1, replica_groups=mesh['replica'=8,'expert'=8,'fsdp'=8] {'replica'}, dimensions={0} | all-to-all | bytes 64 | tf_op jit(solution)/shard_map/all_to_all | solution.py:74
  91.4 2.1 %reshape.90 = bf16[4,34,2048]{2,1,0:T(8,128)(2,1)} reshape(bf16[136,2048]{1,0:T(8,128)(2,1)} %collective-permute-done) | data formatting | bytes 1114112 | tf_op jit(solution)/shard_map/reshape | solution.py:95
  93.5 4.2 %all-to-all-start.3 = ((bf16[4,34,2048]{2,1,0:T(8,128)(2,1)}), bf16[4,34,2048]{2,1,0:T(8,128)(2,1)}, u32[]{:S(2)}, u32[]{:S(2)}) async-start(bf16[4,34,2048]{2,1,0:T(8,128)(2,1)} %reshape.90), calls=%async_computation.3 | async-start | bytes 1310720 | tf_op jit(solution)/shard_map/all_to_all | solution.py:31
  97.6 3.8 %fusion = (bf16[128,6144]{1,0:T(8,128)(2,1)}, bf16[128,6144]{1,0:T(8,128)(2,1)}) fusion(bf16[128,6144]{1,0:T(8,128)(2,1)} %param.9, f32[128]{0:T(128)S(1)} %bitcast.52, f32[128]{0:T(128)S(1)} %get-tuple-element.38), kind=kLoop, calls=%fused_computation.2 | loop fusion | flops 3932160 | bytes 4719616 | tf_op jit(solution)/shard_map/convert_element_type | solution.py:122
  102.5 2.2 %copy.26 = bf16[4,34,6144]{2,1,0:T(8,128)(2,1)} copy(bf16[4,34,6144]{2,0,1:T(4,128)(2,1)S(1)} %dynamic-slice_bitcast_fusion) | data formatting | bytes 3342336 | tf_op jit(solution)/shard_map/dynamic_slice | solution.py:93
  104.7 4.8 %collective-permute-start.4 = (f32[1,1]{1,0:T(1,128)}, f32[1,1]{1,0:T(1,128)}, u32[]{:S(2)}, u32[]{:S(2)}) collective-permute-start(f32[1,1]{1,0:T(1,128)} %bitcast.10), channel_id=1, source_target_pairs={{0,16},{8,24},{16,0},{24,8},{32,48},{40,56},{48,32},{56,40},{1,17}... | collective-permute-start | bytes 20 | tf_op jit(solution)/shard_map/ppermute | solution.py:39
  112.3 4.0 %collective-permute-start.5 = (f32[1,1]{1,0:T(1,128)}, f32[1,1]{1,0:T(1,128)}, u32[]{:S(2)}, u32[]{:S(2)}) collective-permute-start(f32[1,1]{1,0:T(1,128)} %add.75), channel_id=1, source_target_pairs={{0,8},{8,0},{16,24},{24,16},{32,40},{40,32},{48,56},{56,48},{1,9},... | collective-permute-start | bytes 20 | tf_op jit(solution)/shard_map/ppermute | solution.py:39
  117.7 4.4 %all-to-all-start.2 = ((bf16[4,34,6144]{2,1,0:T(8,128)(2,1)}), bf16[4,34,6144]{2,1,0:T(8,128)(2,1)}, u32[]{:S(2)}, u32[]{:S(2)}) async-start(bf16[4,34,6144]{2,1,0:T(8,128)(2,1)} %copy.26), calls=%async_computation.2 | async-start | bytes 3932160 | tf_op jit(solution)/shard_map/all_to_all | solution.py:31
  122.9 2.0 %reshape.91 = bf16[136,2048]{1,0:T(8,128)(2,1)} reshape(bf16[4,34,2048]{2,1,0:T(8,128)(2,1)} %all-to-all-done.3) | data formatting | bytes 1114112 | tf_op jit(solution)/shard_map/reshape | solution.py:95
  126.8 18.1 %all-to-all-done.2 = bf16[4,34,6144]{2,1,0:T(8,128)(2,1)} async-done(((bf16[4,34,6144]{2,1,0:T(8,128)(2,1)}), bf16[4,34,6144]{2,1,0:T(8,128)(2,1)}, u32[]{:S(2)}, u32[]{:S(2)}) %all-to-all-start.2) | async-done | bytes 1671200 | tf_op jit(solution)/shard_map/all_to_all | solution.py:31
  144.9 3.3 %reshape.89 = bf16[136,6144]{1,0:T(8,128)(2,1)} reshape(bf16[4,34,6144]{2,1,0:T(8,128)(2,1)} %all-to-all-done.2) | data formatting | bytes 3342336 | tf_op jit(solution)/shard_map/reshape | solution.py:94
  148.1 3.7 %fusion.20 = f32[256]{0:T(256)S(1)} fusion(bf16[136,6144]{1,0:T(8,128)(2,1)} %reshape.89, bf16[128,6144]{1,0:T(8,128)(2,1)} %get-tuple-element.41, bf16[128,6144]{1,0:T(8,128)(2,1)} %get-tuple-element.40, s32[256]{0:T(256)S(1)} %get-tuple-element.45), kind=kOutput, calls=%fused_computation.18 | convolution fusion | flops 434214656 | bytes 4818944 | tf_op jit(solution)/shard_map/dot_general | solution.py:128
  151.9 30.4 %collective-permute-done.3 = bf16[136,4096]{1,0:T(8,128)(2,1)} collective-permute-done((bf16[136,4096]{1,0:T(8,128)(2,1)}, bf16[136,4096]{1,0:T(8,128)(2,1)}, u32[]{:S(2)}, u32[]{:S(2)}) %collective-permute-start.3) | collective-permute-done | bytes 1114144 | tf_op jit(solution)/shard_map/ppermute | solution.py:36
  182.3 2.1 %fusion.17 = f32[256]{0:T(256)S(1)} fusion(bf16[136,4096]{1,0:T(8,128)(2,1)} %collective-permute-done.3, bf16[128,6144]{1,0:T(8,128)(2,1)S(1)} %copy-done.2, bf16[128,6144]{1,0:T(8,128)(2,1)S(1)} %copy-done.1, s32[256]{0:T(256)S(1)} %get-tuple-element.44), kind=kOutput, calls=%fused_computation.17 | convolution fusion | flops 289511168 | bytes 4261888 | tf_op jit(solution)/shard_map/dot_general | solution.py:128
  (44 shorter events, 13.1 us)
Async XLA Ops:
  0.6 2.0 %copy-start = (bf16[1,1,1,8,34,6144]{5,3,4,2,1,0:T(8,128)(2,1)S(1)}, bf16[1,1,1,8,34,6144]{5,3,4,2,1,0:T(8,128)(2,1)}, u32[]{:S(2)}) copy-start(bf16[1,1,1,8,34,6144]{5,3,4,2,1,0:T(8,128)(2,1)} %param.10) | copy-start | bytes 10027012
  6.1 67.2 %collective-permute-start = (bf16[136,2048]{1,0:T(8,128)(2,1)}, bf16[136,2048]{1,0:T(8,128)(2,1)}, u32[]{:S(2)}, u32[]{:S(2)}) collective-permute-start(bf16[136,2048]{1,0:T(8,128)(2,1)} %reshape.86), channel_id=1, source_target_pairs={{0,32},{8,40},{16,48},{24,56},{32,0},{40,8},{48,16},{56,24},{1,33}... | collective-permute-start | bytes 1671176 | tf_op jit(solution)/shard_map/ppermute | solution.py:36
  23.1 4.5 %copy-start.3 = (f32[1,2,6144]{2,1,0:T(2,128)S(1)}, f32[1,2,6144]{2,1,0:T(2,128)}, u32[]{:S(2)}) copy-start(f32[1,2,6144]{2,1,0:T(2,128)} %param.14) | copy-start | bytes 147460
  23.1 4.5 %copy-start.4 = (f32[2,6144]{1,0:T(2,128)S(1)}, f32[2,6144]{1,0:T(2,128)}, u32[]{:S(2)}) copy-start(f32[2,6144]{1,0:T(2,128)} %param.13) | copy-start | bytes 147460
  23.1 34.5 %copy-start.6 = (s32[128,2]{0,1:T(2,128)S(1)}, s32[128,2]{0,1:T(2,128)}, u32[]{:S(2)}) copy-start(s32[128,2]{0,1:T(2,128)} %param.12) | copy-start | bytes 3076
  23.1 35.2 %copy-start.8 = (f32[4]{0:T(128)S(1)}, f32[4]{0:T(128)}, u32[]{:S(2)}) copy-start(f32[4]{0:T(128)} %param.17) | copy-start | bytes 52
  23.1 40.6 %all-to-all-start = ((bf16[4,34,4096]{2,1,0:T(8,128)(2,1)}), bf16[4,34,4096]{2,1,0:T(8,128)(2,1)}, u32[]{:S(2)}, u32[]{:S(2)}) async-start(bf16[4,34,4096]{2,1,0:T(8,128)(2,1)} %copy.24), calls=%async_computation | async-start | bytes 2621440 | tf_op jit(solution)/shard_map/all_to_all | solution.py:31
  27.6 63.8 %copy-start.7 = (f32[128,2]{0,1:T(2,128)S(1)}, f32[128,2]{0,1:T(2,128)}, u32[]{:S(2)}) copy-start(f32[128,2]{0,1:T(2,128)} %param.11) | copy-start | bytes 3076
  52.8 6.9 %collective-permute-start.1 = (f32[1,1]{1,0:T(1,128)}, f32[1,1]{1,0:T(1,128)}, u32[]{:S(2)}, u32[]{:S(2)}) collective-permute-start(f32[1,1]{1,0:T(1,128)} %bitcast.2), channel_id=1, source_target_pairs={{0,16},{8,24},{16,0},{24,8},{32,48},{40,56},{48,32},{56,40},{1,17}... | collective-permute-start | bytes 20 | tf_op jit(solution)/shard_map/ppermute | solution.py:39
  61.1 12.3 %collective-permute-start.2 = (f32[1,1]{1,0:T(1,128)}, f32[1,1]{1,0:T(1,128)}, u32[]{:S(2)}, u32[]{:S(2)}) collective-permute-start(f32[1,1]{1,0:T(1,128)} %add.65), channel_id=1, source_target_pairs={{0,0},{8,8},{16,48},{24,56},{1,1},{9,9},{17,49},{25,57},{2,2},{10,... | collective-permute-start | bytes 20 | tf_op jit(solution)/shard_map/ppermute | solution.py:47
  73.3 108.9 %collective-permute-start.3 = (bf16[136,4096]{1,0:T(8,128)(2,1)}, bf16[136,4096]{1,0:T(8,128)(2,1)}, u32[]{:S(2)}, u32[]{:S(2)}) collective-permute-start(bf16[136,4096]{1,0:T(8,128)(2,1)} %reshape.87), channel_id=1, source_target_pairs={{0,32},{8,40},{16,48},{24,56},{32,0},{40,8},{48,16},{56,24},{1,33}... | collective-permute-start | bytes 3342344 | tf_op jit(solution)/shard_map/ppermute | solution.py:36
  93.5 24.3 %all-to-all-start.3 = ((bf16[4,34,2048]{2,1,0:T(8,128)(2,1)}), bf16[4,34,2048]{2,1,0:T(8,128)(2,1)}, u32[]{:S(2)}, u32[]{:S(2)}) async-start(bf16[4,34,2048]{2,1,0:T(8,128)(2,1)} %reshape.90), calls=%async_computation.3 | async-start | bytes 1310720 | tf_op jit(solution)/shard_map/all_to_all | solution.py:31
  104.7 6.3 %collective-permute-start.4 = (f32[1,1]{1,0:T(1,128)}, f32[1,1]{1,0:T(1,128)}, u32[]{:S(2)}, u32[]{:S(2)}) collective-permute-start(f32[1,1]{1,0:T(1,128)} %bitcast.10), channel_id=1, source_target_pairs={{0,16},{8,24},{16,0},{24,8},{32,48},{40,56},{48,32},{56,40},{1,17}... | collective-permute-start | bytes 20 | tf_op jit(solution)/shard_map/ppermute | solution.py:39
  112.3 4.7 %collective-permute-start.5 = (f32[1,1]{1,0:T(1,128)}, f32[1,1]{1,0:T(1,128)}, u32[]{:S(2)}, u32[]{:S(2)}) collective-permute-start(f32[1,1]{1,0:T(1,128)} %add.75), channel_id=1, source_target_pairs={{0,8},{8,0},{16,24},{24,16},{32,40},{40,32},{48,56},{56,48},{1,9},... | collective-permute-start | bytes 20 | tf_op jit(solution)/shard_map/ppermute | solution.py:39
  117.7 4.5 %copy-start.5 = (f32[2,6144]{1,0:T(2,128)S(1)}, f32[2,6144]{1,0:T(2,128)}, u32[]{:S(2)}) copy-start(f32[2,6144]{1,0:T(2,128)} %param.15) | copy-start | bytes 147460
  117.7 27.2 %all-to-all-start.2 = ((bf16[4,34,6144]{2,1,0:T(8,128)(2,1)}), bf16[4,34,6144]{2,1,0:T(8,128)(2,1)}, u32[]{:S(2)}, u32[]{:S(2)}) async-start(bf16[4,34,6144]{2,1,0:T(8,128)(2,1)} %copy.26), calls=%async_computation.2 | async-start | bytes 3932160 | tf_op jit(solution)/shard_map/all_to_all | solution.py:31
  148.1 34.1 %copy-start.1 = (bf16[128,6144]{1,0:T(8,128)(2,1)S(1)}, bf16[128,6144]{1,0:T(8,128)(2,1)}, u32[]{:S(2)}) copy-start(bf16[128,6144]{1,0:T(8,128)(2,1)} %get-tuple-element.40) | copy-start | bytes 4718596
  148.1 34.1 %copy-start.2 = (bf16[128,6144]{1,0:T(8,128)(2,1)S(1)}, bf16[128,6144]{1,0:T(8,128)(2,1)}, u32[]{:S(2)}) copy-start(bf16[128,6144]{1,0:T(8,128)(2,1)} %get-tuple-element.41) | copy-start | bytes 4718596
